TPU v7x, 32 devices: a whole 2x2x4 slice. The times are simulated.
32 devices in a mesh: ha: 2 (over core), wa: 2 (over x), batch: 8 (over z, y).
Axes of the slice: x: 2, y: 2, z: 4, core: 2. Of those that a mesh axis runs over, the one named last changes fastest.
Arguments:
- inputs: bfloat16 [2, 128, 8, 8, 512], P(None, 'batch', 'ha', 'wa'), may hold values from -22 to 22
- starts: int32 [2, 128], P(None, 'batch'), may hold values from 0 to 1, as said below
- first_spatial: bfloat16 [4608, 1152], P('batch'), may hold values from -0.09375 to 0.09375
- first_mid_gain: bfloat16 [1152], P('batch'), may hold values from 0.5 to 1.5
- first_mid_bias: bfloat16 [1152], P('batch'), may hold values from -3 to 3
- first_temporal: bfloat16 [3456, 512], P('batch'), may hold values from -0.109375 to 0.109375
- first_out_gain: bfloat16 [512], P('batch'), may hold values from 0.5 to 1.5
- first_out_bias: bfloat16 [512], P('batch'), may hold values from -3 to 3
- second_spatial: bfloat16 [4608, 1152], P('batch'), may hold values from -0.09375 to 0.09375
- second_mid_gain: bfloat16 [1152], P('batch'), may hold values from 0.5 to 1.5
- second_mid_bias: bfloat16 [1152], P('batch'), may hold values from -3 to 3
- second_temporal: bfloat16 [3456, 512], P('batch'), may hold values from -0.109375 to 0.109375
- second_out_gain: bfloat16 [512], P('batch'), may hold values from 0.5 to 1.5
- second_out_bias: bfloat16 [512], P('batch'), may hold values from -3 to 3
- cotangent: bfloat16 [2, 128, 8, 8, 512], P(None, 'batch', 'ha', 'wa'), may hold values from -22 to 22
Outputs:
- block_out: float32 [2, 128, 8, 8, 512], P(None, 'batch', 'ha', 'wa')
- grad_input: float32 [2, 128, 8, 8, 512], P(None, 'batch', 'ha', 'wa')
- grad_first_spatial: float32 [4608, 1152], P('batch')
- grad_first_mid_gain: float32 [1152], P('batch')
- grad_first_mid_bias: float32 [1152], P('batch')
- grad_first_temporal: float32 [3456, 512], P('batch')
- grad_first_out_gain: float32 [512], P('batch')
- grad_first_out_bias: float32 [512], P('batch')
- grad_second_spatial: float32 [4608, 1152], P('batch')
- grad_second_mid_gain: float32 [1152], P('batch')
- grad_second_mid_bias: float32 [1152], P('batch')
- grad_second_temporal: float32 [3456, 512], P('batch')
- grad_second_out_gain: float32 [512], P('batch')
- grad_second_out_bias: float32 [512], P('batch')
Inputs may be any that keep to these rules, and one draw needn't show every extreme that they name: `starts`: 1 marks the first frame of a clip within its micro-batch; no temporal tap joins frames of different clips or micro-batches.
All inputs are finite; a program needn't handle non-finite values.
Results may differ from a plain program's by a relative error of at most 0.017.
Values may be sent and summed in bfloat16 or wider, within the bound.
A program may use at most 256 MiB of HBM per device.

v0:
```python
import functools
from types import SimpleNamespace

import jax
import jax.numpy as jnp
from jax import lax
from jax.experimental import pallas as pl
from jax.experimental.pallas import tpu as pltpu
from jax.sharding import PartitionSpec as P

HGT = 7
epsilon = 1e-05
MESH = pl.DeviceIdType.MESH
F32 = jnp.float32
BF16 = jnp.bfloat16

BASE = 10
CELL = 8
ROWS = HGT * 8 * CELL
PADDED = (BASE + HGT * 8 + BASE) * CELL
MAIN = BASE * CELL
CHUNK = 2 * CELL
CHUNKS = ROWS // CHUNK
VMEM_LIMIT = 64 * 1024 * 1024 - 1024 * 1024


def when(cond, work):
    if cond is True:
        work()
    elif cond is not False:
        pl.when(cond)(work)


def loop(count, body, init):
    def twice(i, carry):
        return body(2 * i + 1, body(2 * i, carry))

    return lax.fori_loop(0, count // 2, twice, init)


def sigmoid(x):
    return 0.5 * jnp.tanh(0.5 * x) + 0.5


def nn(a, b):
    return jnp.dot(a, b, preferred_element_type=F32)


def nt(a, b):
    return lax.dot_general(a, b, (((1,), (1,)), ((), ())), preferred_element_type=F32)


def tn(a, b):
    return lax.dot_general(a, b, (((0,), (0,)), ((), ())), preferred_element_type=F32)


def rows_of(start, size, step=16):
    if not isinstance(start, int):
        start = pl.multiple_of(start, step)
    return pl.ds(start, size)


def block_kernel(dims, names, *all_refs):
    r = SimpleNamespace(**dict(zip(names, all_refs, strict=True)))
    nb, chan, mid, cell_count = dims
    spat = 9 * chan // nb
    temp = 3 * mid // nb
    unit = spat // 6
    quarter = chan // 4
    half = chan // 2
    h = lax.axis_index("ha")
    w = lax.axis_index("wa")
    b = lax.axis_index("batch")
    par = lax.rem(b, 2)
    bh = lax.div(b, 2)
    pos = par * (nb - 1 - bh) + (1 - par) * bh

    def at(p):
        p = lax.rem(p + 4 * nb, nb)
        upper = lax.div(p, nb // 2)
        return (1 - upper) * (2 * p) + upper * (2 * (nb - 1 - p) + 1)

    def at_group(j):
        return (lax.rem(j, 2), lax.div(j, 2))

    mine = 2 * w + h
    sibling = (1 - h, w, b)
    beside = (h, 1 - w, b)
    later_dev = (1 - h, w, lax.rem(b + h, nb))
    earlier_dev = (1 - h, w, lax.rem(b + nb - 1 + h, nb))
    tile_group = [(lax.rem(mine + d, 4), (*at_group(lax.rem(mine + d, 4)), b)) for d in (1, 2, 3)]
    across = (h, w, b + 1 - 2 * par)
    pos_b = h * 2 + par
    plane = []
    for d in (1, 2, 3):
        q = lax.rem(pos_b + d, 4)
        plane.append((q, (lax.div(q, 2), w, b - par + lax.rem(q, 2))))
    depth = nb // 2
    line = []
    for d in range(1, depth):
        q = lax.rem(bh + d, depth)
        line.append((q, (h, w, 2 * q + par)))

    def named(dev):
        return dict(ha=dev[0], wa=dev[1], batch=dev[2])

    def rc(src, dst, send, recv, dev):
        return pltpu.make_async_remote_copy(
            src_ref=src, dst_ref=dst, send_sem=send, recv_sem=recv, device_id=named(dev), device_id_type=MESH
        )

    def lc(src, dst, sem):
        return pltpu.make_async_copy(src, dst, sem)

    partners = [sibling, beside, (h, w, at(pos + 1)), (h, w, at(pos - 1)), later_dev, earlier_dev]
    partners += [dev for _, dev in tile_group + plane + line]
    barrier = pltpu.get_barrier_semaphore()
    for dev in partners:
        pl.semaphore_signal(barrier, inc=1, device_id=named(dev), device_id_type=MESH)
    pl.semaphore_wait(barrier, len(partners))

    shards = (r.first_spatial, r.first_temporal, r.second_spatial, r.second_temporal)
    whole = ((r.w1s0, r.w1s1), (r.w1t0, r.w1t1), (r.w2s0, r.w2s1), (r.w2t0, r.w2t1))
    halves = ((0, 512), (512, mid - 512))
    shared = 2 * w + h
    shared_beside = 2 * (1 - w) + h
    way = 1 - 2 * h
    onward = (h, w, at(pos + way))
    third = temp // 3

    def taken(i, core, side):
        if i % 2 == 0:
            return 3 * unit * core + unit * side, 2 * unit
        return (1 - core) * 2 * third * side + core * third, third

    def crosses(i, core, side):
        if i % 2 == 0:
            return 3 * unit * core + 2 * unit * side, unit
        return 2 * third * side, third

    def rows_in(i, c, owner, part):
        size = spat if i % 2 == 0 else temp
        return whole[i][c].at[rows_of(owner * size + part[0], part[1]), :]

    def rows_from(i, c, part):
        c0, cw = halves[c] if i % 2 == 0 else (c * half, half)
        return shards[i].at[rows_of(part[0], part[1]), c0 : c0 + cw]

    def pieces(i):
        start, size = taken(i, h, w)
        if i:
            return ((start, size),)
        return ((start, size // 2), (start + size // 2, size // 2))

    def crossing(i, work):
        if i % 2 == 0:
            work()
        else:
            pl.when(h == 0)(work)

    def own_copy(i, c):
        rows = spat if i % 2 == 0 else temp
        return lc(rows_from(i, c, (0, rows)), rows_in(i, c, b, (0, rows)), r.own_sem.at[i, c])

    def ring(i, c, k, s, owner, from_shard=False):
        part = pieces(i)[k]
        dst = rows_in(i, c, owner, part)
        src = rows_from(i, c, part) if from_shard else dst
        return rc(src, dst, r.ring_send.at[i, c], r.ring_recv.at[i, c, k, s], onward)

    def cross(i, c, owner, part):
        ref = rows_in(i, c, owner, part)
        return rc(ref, ref, r.sib_send.at[i, c], r.sib_recv.at[i, c], sibling)

    def over(i, c, s, owner, part):
        ref = rows_in(i, c, owner, part)
        return rc(ref, ref, r.over_send.at[i, c], r.over_recv.at[i, c, s], beside)

    def gather_start(i):
        for k in range(len(pieces(i))):
            for c in (0, 1):
                ring(i, c, k, 1, b, True).start()
        for c in (0, 1):
            own_copy(i, c).start()

    def gather_relay(i, s):
        owner = at(pos - way * s)

        def work():
            part = crosses(i, h, 1 - w)
            for c in (0, 1):
                over(i, c, s, owner, part).wait_recv()
                cross(i, c, owner, part).start()

        crossing(i, work)

    def gather_pump(i, s):
        owner = at(pos - way * s)
        for k in range(len(pieces(i))):
            for c in (0, 1):
                ring(i, c, k, s, owner).wait_recv()
                if isinstance(s, int):
                    if s < nb - 1:
                        ring(i, c, k, s + 1, owner).start()
                else:
                    pl.when(s < nb - 1)(lambda k=k, c=c: ring(i, c, k, s + 1, owner).start())
        for c in (0, 1):
            crossing(i, lambda c=c: over(i, c, s, owner, crosses(i, h, w)).start())
            cross(i, c, owner, taken(i, h, w)).start()
        if isinstance(s, int):
            if s > 1:
                gather_relay(i, s - 1)
        else:
            pl.when(s > 1)(lambda: gather_relay(i, s - 1))

    def span(i, c, size):
        return whole[i][c].at[0 : (nb - 1) * size, :]

    def gather_finish(i):
        gather_relay(i, nb - 1)

        def arrived(size):
            for c in (0, 1):
                ref = span(i, c, size)
                rc(ref, ref, r.sib_send.at[i, c], r.sib_recv.at[i, c], sibling).wait_recv()

        if i % 2 == 0:
            arrived(3 * unit)
        else:
            pl.when(h == 0)(lambda: arrived(third))
            pl.when(h == 1)(lambda: arrived(2 * third))
        for c in (0, 1):
            own_copy(i, c).wait()

    def gather_sent(i):
        def sent(size, sem):
            for c in (0, 1):
                ref = span(i, c, size)
                rc(ref, ref, sem.at[i, c], r.own_sem.at[i, c], sibling).wait_send()

        sent(taken(i, h, w)[1], r.ring_send)
        crossing(i, lambda: sent(crosses(i, h, w)[1], r.over_send))
        if i % 2 == 0:
            sent(3 * unit, r.sib_send)
        else:
            pl.when(h == 0)(lambda: sent(2 * third, r.sib_send))
            pl.when(h == 1)(lambda: sent(third, r.sib_send))

    def total(k, width, value, works=()):
        slot = k % 2
        wide = value.shape[1]
        cols = pl.ds(0, wide)
        works = list(works) + [None] * 2
        four, far = r.sum_b, r.sum_c
        four[slot, pos_b, :, cols] = value

        def phase(ref, me, group, send, recv, work):
            for _, dev in group:
                part = ref.at[slot, me, :, cols]
                rc(part, part, send.at[k], recv.at[k], dev).start()
            if work:
                work()
            ref = ref.at[slot, 0 : len(group), :, cols]
            every = rc(ref, ref, send.at[k], recv.at[k], sibling)
            every.wait_recv()
            return every

        first = phase(four, pos_b, plane, r.sb_send, r.sb_recv, works[0])
        far[slot, bh, :, cols] = (four[slot, 0, :, cols] + four[slot, 1, :, cols]) + (
            four[slot, 2, :, cols] + four[slot, 3, :, cols]
        )
        second = phase(far, bh, line, r.sc_send, r.sc_recv, works[1])
        result = far[slot, 0, :, cols]
        for q in range(1, depth):
            result = result + far[slot, q, :, cols]
        first.wait_send()
        second.wait_send()
        if wide == width:
            return result
        return jnp.concatenate([result[2 * n : 2 * n + 2] for n in range(width // wide)], axis=1)

    def chunk(ref, i, base=0, width=None):
        cols = slice(None) if width is None else pl.ds(0, width)
        value = ref[rows_of(base + i * CHUNK, CHUNK), cols]
        return value.astype(F32).reshape(2, CELL, value.shape[-1])

    def put(ref, i, value, base=0, width=None):
        cols = slice(None) if width is None else pl.ds(0, width)
        ref[rows_of(base + i * CHUNK, CHUNK), cols] = value.reshape(CHUNK, value.shape[-1]).astype(ref.dtype)

    def keep(i):
        inside = jnp.where(lax.rem(i, 4) == 3, 0.0, 1.0).astype(F32)
        first = lax.broadcasted_iota(jnp.int32, (2, 1, 1), 0) == 0
        return jnp.where(first, 1.0, inside)

    def packed(one, two, width):
        rows = jnp.concatenate([jnp.sum(v, axis=0, keepdims=True) for v in (one, two)], axis=0)
        wide = 384 if width == mid else 128
        parts = [rows[:, n * wide : (n + 1) * wide] for n in range(width // wide)]
        return jnp.concatenate((parts + parts[-1:])[0:4], axis=0)

    def moments(ref, width):
        def body(i, carry):
            v = chunk(ref, i)
            m = v * keep(i)
            return (carry[0] + m[0] + m[1], carry[1] + m[0] * v[0] + m[1] * v[1])

        zero = jnp.zeros((CELL, width), F32)
        return loop(CHUNKS, body, (zero, zero))

    def prepare(n, sums, width):
        tile = r.tile_mid if width == mid else r.tile_out
        n2 = n // 2
        gain = r.param[2 * n : 2 * n + 1, 0:width]
        bias = r.param[2 * n + 1 : 2 * n + 2, 0:width]
        mean = sums[0:1] / cell_count
        inv = lax.rsqrt(sums[1:2] / cell_count - mean * mean + epsilon)
        scale = inv * gain
        shift = bias - mean * scale
        for k, v in enumerate((scale, shift, inv, mean * inv)):
            tile[n2, k] = jnp.broadcast_to(v, (CELL, width))

    def tiles(n, width):
        tile = r.tile_mid if width == mid else r.tile_out
        return [tile[n // 2, k][None] for k in range(4)]

    def fill(ref_a, ref_b, value_of, width):
        pads(ref_a, ref_b, width)

        def body(i, before):
            v = value_of(i)
            put(ref_a, i, v, MAIN)
            pair = jnp.concatenate([before[None], v[0:1]], axis=0)
            put(ref_b, i, pair, MAIN - CHUNK)
            return v[1]

        loop(CHUNKS, body, jnp.zeros((CELL, width), F32))

    def activated(src, n, width):
        def value(i):
            scale, shift, _, _ = tiles(n, width)
            y = chunk(src, i) * scale + shift
            return y * sigmoid(y) * keep(i)

        return value

    def taps(ref_a, ref_b, k, size=ROWS):
        r0 = MAIN - 8 * CELL + 8 * CELL * k
        return (
            ref_b[rows_of(r0 - CHUNK, size), :],
            ref_a[rows_of(r0, size), :],
            ref_b[rows_of(r0, size), :],
        )

    def conv(ref_a, ref_b, weight, out, pump=None):
        for n, (c0, cw) in enumerate(halves):

            def body(a, _, c0=c0, cw=cw, n=n):
                x = taps(ref_a, ref_b, a)
                acc = nn(jnp.concatenate(x, axis=1), weight[n][rows_of(a * 3 * chan, 3 * chan), :])

                @pl.when(a == 0)
                def _():
                    out[:, c0 : c0 + cw] = acc

                @pl.when(a > 0)
                def _():
                    out[:, c0 : c0 + cw] += acc

                if pump is not None:
                    pump(n * 3 + a)
                return 0

            lax.fori_loop(0, 3, body, 0)

    def conv_back(ref_a, ref_b, weight, out, pump=None):
        def body(k, _):
            e = taps(ref_a, ref_b, k)
            acc = None
            for j in range(3):
                tap = 8 - 3 * k - j
                for n, (c0, cw) in enumerate(halves):
                    term = nt(e[j][:, c0 : c0 + cw], weight[n][rows_of(tap * chan, chan), :])
                    acc = term if acc is None else acc + term

            @pl.when(k == 0)
            def _():
                out[:, 0:chan] = acc

            @pl.when(k > 0)
            def _():
                out[:, 0:chan] += acc

            if pump is not None:
                pump(k)
            return 0

        lax.fori_loop(0, 3, body, 0)

    def send_frames(k):
        down, up = r.down, r.up
        count = ROWS // CELL
        for c in range(chan // 128):
            lanes = pl.ds(128 * c, 128)
            r.halo_out[0, :, lanes] = down[c, pl.ds(2 * CELL - 1, count, stride=CELL), :]
            r.halo_out[1, :, lanes] = up[c, pl.ds(0, count, stride=CELL), :]
        copies = []
        for n, dev in ((0, later_dev), (1, earlier_dev)):
            copies.append(
                rc(r.halo_out.at[n], r.halo_in.at[k, n], r.halo_send.at[k, n], r.halo_recv.at[k, n], dev)
            )
            copies[-1].start()
        return copies

    def take_frames(k, copies):
        down, up = r.down, r.up
        count = ROWS // CELL
        for copy in copies:
            copy.wait()
        at_start = jnp.logical_and(h == 0, b == 0)
        at_end = jnp.logical_and(h == 1, b == nb - 1)
        for c in range(chan // 128):
            lanes = pl.ds(128 * c, 128)
            before = r.halo_in[k, 0, :, lanes]
            after = r.halo_in[k, 1, :, lanes]
            down[c, pl.ds(CELL - 1, count, stride=CELL), :] = jnp.where(at_start, 0.0, before)
            up[c, pl.ds(CELL, count, stride=CELL), :] = jnp.where(at_end, 0.0, after)

    def by_lanes(ref, rows):
        return jnp.concatenate([ref[c, rows, :] for c in range(chan // 128)], axis=1)

    def put_lanes(ref, rows, value):
        for c in range(chan // 128):
            ref[c, rows, :] = value[:, 128 * c : 128 * c + 128]

    def shifted(i):
        before = by_lanes(r.down, rows_of(i * CHUNK, CHUNK + CELL))[CELL - 1 : CELL - 1 + CHUNK]
        after = by_lanes(r.up, rows_of(i * CHUNK, CHUNK + CELL))[1 : 1 + CHUNK]
        gate = r.gate[...][None]
        return (before.reshape(2, CELL, chan) * gate, after.reshape(2, CELL, chan))

    def both_halves(weight, start, size):
        return jnp.concatenate([part[start : start + size, :] for part in weight], axis=1)

    def temporal(k, v, weight, out, works=()):
        works = list(works) + [None] * 2
        put_lanes(r.down, pl.ds(CELL, ROWS), nn(v[...], both_halves(weight, 0, mid)))
        y2 = nn(v[...], both_halves(weight, 2 * mid, mid))
        y2 = (y2.reshape(ROWS // CELL, CELL, chan) * r.gate[...][None]).reshape(ROWS, chan)
        put_lanes(r.up, pl.ds(0, ROWS), y2)
        copies = send_frames(k)
        out[...] = nn(v[...], both_halves(weight, mid, mid))
        if works[0]:
            works[0]()
        take_frames(k, copies)

        def body(i, carry):
            before, after = shifted(i)
            value = chunk(out, i) + before + after
            put(out, i, value)
            m = value * keep(i)
            return (carry[0] + m[0] + m[1], carry[1] + m[0] * value[0] + m[1] * value[1])

        zero = jnp.zeros((CELL, chan), F32)
        return loop(CHUNKS, body, (zero, zero))

    def put_e(tap, i, e):
        for c in (0, 1):
            r.e3[c, tap, rows_of(i * CHUNK, CHUNK), :] = e[:, c * half : (c + 1) * half]

    def temporal_back(k, weight, works=()):
        works = list(works) + [None] * 2
        copies = send_frames(k)
        e3 = r.e3

        def e_tap(n):
            return jnp.concatenate([e3[0, n], e3[1, n]], axis=1)

        for c0, cw in ((0, 512), (512, mid - 512)):
            r.grad_mid[:, c0 : c0 + cw] = nt(e_tap(1), both_halves(weight, mid + c0, cw))
        if works[0]:
            works[0]()
        take_frames(k, copies)

        def body(i, _):
            before, after = shifted(i)
            put_e(0, i, after.reshape(CHUNK, chan).astype(BF16))
            put_e(2, i, before.reshape(CHUNK, chan).astype(BF16))
            return 0

        loop(CHUNKS, body, 0)
        share = share_e3(k)
        for c0, cw in ((0, 512), (512, mid - 512)):
            r.grad_mid[:, c0 : c0 + cw] += nt(e_tap(0), both_halves(weight, c0, cw)) + nt(
                e_tap(2), both_halves(weight, 2 * mid + c0, cw)
            )
        return share

    def share(k, src, dst):
        copy = rc(src, dst, r.share_send.at[k], r.share_recv.at[k], sibling)
        copy.start()
        return copy

    outs = ((r.out1s0, r.out1s1), r.out1t, (r.out2s0, r.out2s1), r.out2t)

    e_all = (r.e_all0, r.e_all1)

    def e_part(n, slot):
        return e_all[n].at[slot * ROWS : (slot + 1) * ROWS, :]

    def e_copies(k, n):
        send, near, over = r.e_send.at[k, n], r.e_recv.at[k, n, 0], r.e_recv.at[k, n, 1]
        return [
            rc(e_part(n, 0), e_part(n, 1), send, near, sibling),
            rc(e_part(n, 0), e_part(n, 2), send, over, beside),
            rc(e_part(n, 2), e_part(n, 3), send, near, sibling),
        ]

    def share_e(k):
        for n in (0, 1):
            near, over, _ = e_copies(k, n)
            over.start()
            near.start()

    def share_e_on(k, n):
        _, over, far = e_copies(k, n)
        over.wait_recv()
        far.start()

    def share_e_wait(k, n):
        both = e_all[n].at[0 : 2 * ROWS, :]
        rc(both, both, r.e_send.at[k, n], r.e_recv.at[k, n, 0], sibling).wait_recv()
        three = e_all[n].at[0 : 3 * ROWS, :]
        rc(three, three, r.e_send.at[k, n], r.e_recv.at[k, n, 0], sibling).wait_send()

    def share_x(k, xa, xq):
        main = pl.ds(MAIN, ROWS)
        for n, dev in enumerate((sibling, beside, (1 - h, 1 - w, b))):
            lanes = rows_of((2 * dev[1] + dev[0]) * quarter, quarter, 128)
            rc(xa.at[main, lanes], xq.at[n, 0, main, :], r.xq_send.at[k], r.xq_recv.at[k], dev).start()
        all_three = xq.at[:, 0, main, :]
        return rc(all_three, all_three, r.xq_send.at[k], r.xq_recv.at[k], sibling)

    def pads(ref_a, ref_b, width):
        ref_a[0:MAIN, :] = jnp.zeros((MAIN, width), BF16)
        ref_a[MAIN + ROWS : PADDED, :] = jnp.zeros((PADDED - MAIN - ROWS, width), BF16)
        ref_b[0 : MAIN - CHUNK, :] = jnp.zeros((MAIN - CHUNK, width), BF16)
        ref_b[MAIN - CHUNK + ROWS : PADDED, :] = jnp.zeros((PADDED - MAIN + CHUNK - ROWS, width), BF16)

    def spread_x(xq):
        for n in range(3):
            pads(xq.at[n, 0], xq.at[n, 1], quarter)

        def body(i, before):
            after = []
            for n in range(3):
                v = chunk(xq.at[n, 0], i, MAIN)
                put(xq.at[n, 1], i, jnp.concatenate([before[n][None], v[0:1]], axis=0), MAIN - CHUNK)
                after.append(v[1])
            return tuple(after)

        loop(CHUNKS, body, (jnp.zeros((CELL, quarter), F32),) * 3)

    def share_e3(k):
        return share(
            k - 2, r.e3.at[1 - h], r.sib_e3
        )

    def line_row(place):
        return quarter * place + 64 * jnp.where(place > shared, 1, 0)

    def grad_row(tap, side):
        split = 2 * shared + 1
        owner = jnp.where(tap == split, 2 * shared + side, tap - jnp.where(tap > split, 1, 0))
        row = line_row(lax.div(owner, 2)) + jnp.where(tap == split, quarter, 64 * side)
        return 576 * lax.rem(owner, 2) + row

    spare = whole[2]

    def gq(i, row, size):
        return rows_of((mid if i == 0 else 0) + row, size, 64)

    def inbox(i, row, size):
        return rows_of(2 * mid + (mid if i == 0 else 0) + row, size, 64)

    def transpose_x(a, xa, xb, xq, near, far, row):
        lanes = rows_of(shared * quarter, quarter, 128)
        r0 = MAIN - 8 * CELL + 8 * CELL * a
        for j, (c, start) in enumerate(((1, r0 - CHUNK), (0, r0), (1, r0))):
            rows = rows_of(start, ROWS)
            own = (xb if c else xa)[rows, lanes]
            both = jnp.concatenate([own, xq[0, c, rows, :]], axis=0)
            near[rows_of(row + j * quarter, quarter), 0 : 2 * ROWS] = both.T
            both = jnp.concatenate([xq[1, c, rows, :], xq[2, c, rows, :]], axis=0)
            far[rows_of(row + j * quarter, quarter), 0 : 2 * ROWS] = both.T

    def spatial_part(i, near, far, row, tap, n):
        rows = rows_of(row, 3 * quarter)
        acc = nn(near[rows, :], e_all[n][0 : 2 * ROWS, :])
        acc += nn(far[rows, :], e_all[n][2 * ROWS : 4 * ROWS, :])
        acc = acc.astype(BF16)
        for j in range(6):
            spare[n][gq(i, grad_row(tap + j // 2, j % 2), 64), :] = acc[64 * j : 64 * j + 64]

    def transposes(xa, xb, xq, near, far):
        def body(a, _):
            transpose_x(a, xa, xb, xq, near, far, a * 3 * quarter)
            return 0

        lax.fori_loop(0, 3, body, 0)

    def spatial_half(i, near, far, n):
        def body(a, _):
            spatial_part(i, near, far, a * 3 * quarter, 3 * a, n)
            return 0

        lax.fori_loop(0, 3, body, 0)

    def transpose_v(v, sv):
        for c in range(mid // 128):
            lanes = pl.ds(128 * c, 128)
            turned = jnp.concatenate([v[:, lanes], sv[:, lanes]], axis=0).T
            for row in (0, 64):
                ref = r.ea if 128 * c + row < mid // 2 else r.eb
                at_row = (128 * c + row) % (mid // 2)
                ref[at_row : at_row + 64, 0 : 2 * ROWS] = turned[row : row + 64]

    def temporal_grad(i, first, count):
        taps_of = [jnp.concatenate([r.e3[h, k], r.sib_e3[k]], axis=0) for k in range(first, first + count)]
        e = jnp.concatenate(taps_of, axis=1)
        whole_tap = mid // third
        for top in range(0, whole_tap, whole_tap // 2):
            acc = nn((r.eb if top else r.ea)[0 : mid // 2, 0 : 2 * ROWS], e).astype(BF16)
            for k in range(count):
                for n in range(whole_tap // 2):
                    owner, part = divmod((first + k) * whole_tap + top + n, 3)
                    row = (owner % 2) * (depth * temp) + owner // 2 * temp + part * third
                    whole[i][0][row : row + third, :] = acc[n * third : n * third + third, k * half : (k + 1) * half]

    def parts_of(i):
        return (0, 1) if i % 2 == 0 else (0,)

    line_size = 576

    def to_y(i, n, side):
        if i % 2 == 0:
            return spare[n].at[gq(i, line_size * side, line_size), :]
        return whole[i][0].at[rows_of(depth * temp * side, depth * temp), :]

    def y_box(i, n):
        if i % 2 == 0:
            return spare[n].at[inbox(i, 0, line_size), :]
        return whole[i][1].at[0 : depth * temp, :]

    def block_of(i, n, place, size):
        if i % 2 == 0:
            return spare[n].at[gq(i, line_size * par + line_row(place), size), :]
        return whole[i][0].at[rows_of(depth * temp * par + place * temp, temp), :]

    def z_box(i, n, slot, size):
        if i % 2 == 0:
            return spare[n].at[inbox(i, line_size + slot * (line_size // 3), size), :]
        return whole[i][1].at[(depth + slot) * temp : (depth + slot + 1) * temp, :]

    def sized(i, place, work):
        if i % 2:
            work(temp)
        else:
            pl.when(place != shared)(lambda: work(quarter))
            pl.when(place == shared)(lambda: work(quarter + 64))

    def t_inbox(i, n):
        return whole[i][1].at[n * temp : (n + 1) * temp, :]

    def add_into(dst, parts, step):
        rows, cols = dst.shape

        def body(n, _):
            at_rows = rows_of(n * step, step)
            value = dst[at_rows, :].astype(F32)
            for part in parts:
                value = value + part[at_rows, :].astype(F32)
            dst[at_rows, :] = value.astype(BF16)
            return 0

        lax.fori_loop(0, rows // step, body, 0)

    def y_copy(i, n):
        return rc(to_y(i, n, 1 - par), y_box(i, n), r.y_send.at[i, n], r.y_recv.at[i, n], across)

    def z_copy(i, n, d, size):
        place = lax.rem(bh + d, depth)
        dev = (h, w, 2 * place + par)
        src, dst = block_of(i, n, place, size), z_box(i, n, 3 - d, size)
        return rc(src, dst, r.z_send.at[i, n], r.z_recv.at[i, n], dev)

    def step_of(i):
        return 32 if i % 2 == 0 else 48

    def reduce_start(i, n):
        y_copy(i, n).start()

    def reduce_middle(i, n):
        y_copy(i, n).wait()
        add_into(to_y(i, n, par), [y_box(i, n)], step_of(i))
        for d in (1, 2, 3):
            sized(i, lax.rem(bh + d, depth), lambda size, d=d: z_copy(i, n, d, size).start())

    def final_part(i, n, side, core):
        place = 2 * side + core
        start = quarter * place - 64 * b + 512 * jnp.where(b > 2 * place, 1, 0)
        return outs[i][n].at[rows_of(start, quarter, 64), :]

    def extra_part(i, n):
        return outs[i][n].at[rows_of(512 * (1 - par), 64, 64), :]

    def final_copies(i, n):
        if i % 2:
            src = block_of(i, n, bh, temp)
            part = outs[i].at[h]
            return lc(src, part, r.out_sem.at[i, 0, 0]), [
                (src, part, sibling, r.cast_send.at[i, 0, 0], r.cast_recv.at[i, 0, 0])
            ]
        src = block_of(i, n, bh, quarter)
        part = final_part(i, n, w, h)
        sends = [
            (src, part, dev, r.cast_send.at[i, n, d], r.cast_recv.at[i, n, d]) for d, dev in enumerate((beside, sibling))
        ]
        return lc(src, part, r.out_sem.at[i, n, 0]), sends

    def extra_copies(i, n):
        src = spare[n].at[gq(i, line_size * par + line_row(bh) + quarter, 64), :]
        part = extra_part(i, n)
        sends = [
            (src, part, dev, r.cast_send.at[i, n, 3 + d], r.cast_recv.at[i, n, 3 + d])
            for d, dev in enumerate((beside, sibling))
        ]
        return lc(src, part, r.out_sem.at[i, n, 1]), sends

    def begin(copies):
        local, sends = copies
        for src, part, dev, one, two in sends:
            rc(src, part, one, two, dev).start()
        local.start()

    def credit(n):
        pl.semaphore_signal(r.credit.at[n], inc=1, device_id=named(beside), device_id_type=MESH)

    def credited(n):
        pl.semaphore_wait(r.credit.at[n], 1)

    def beside_copy(i):
        return rc(block_of(i, 0, bh, temp), t_inbox(i, 7), r.fin_send.at[i], r.fin_recv.at[i], beside)

    def z_span(i, n, rows):
        return to_y(i, n, 0).at[0:rows, :]

    def reduce_last(i, n):
        def add(size):
            ref = z_span(i, n, 3 * size)
            rc(ref, ref, r.z_send.at[i, n], r.z_recv.at[i, n], across).wait_recv()
            add_into(block_of(i, n, bh, size), [z_box(i, n, slot, size) for slot in range(3)], step_of(i))

        sized(i, bh, add)
        if i % 2:
            credited(i // 2)
            beside_copy(i).start()
            return
        begin(final_copies(i, n))
        pl.when(bh == shared)(lambda: begin(extra_copies(i, n)))

    def reduce_out(i):
        beside_copy(i).wait()
        add_into(block_of(i, 0, bh, temp), [t_inbox(i, 7)], 48)
        begin(final_copies(i, 0))

    def final_on(i, n):
        def move(part, d):
            rc(part, part, r.cast_send.at[i, n, d], r.cast_recv.at[i, n, d], beside).wait_recv()
            rc(part, part, r.cast_send.at[i, n, d + 2], r.cast_recv.at[i, n, d + 2], sibling).start()

        move(final_part(i, n, 1 - w, h), 0)
        pl.when(bh == shared_beside)(lambda: move(extra_part(i, n), 3))

    def reduce_wait(i, n):
        local, sends = final_copies(i, n)
        local.wait()

        def sent(rows):
            ref = z_span(i, n, rows)
            rc(ref, ref, r.z_send.at[i, n], r.z_recv.at[i, n], across).wait_send()

        if i % 2:
            sent(3 * temp)
        else:
            pl.when(bh == shared)(lambda: sent(3 * quarter))
            pl.when(bh != shared)(lambda: sent(3 * quarter + 64))
        if i % 2:
            src, part, dev, one, two = sends[0]
            rc(src, outs[i].at[1 - h], one, two, dev).wait()
            return
        for src, part, dev, one, two in sends:
            rc(src, part, one, two, dev).wait_send()

        def far(part, d):
            return rc(part, part, r.cast_send.at[i, n, d], r.cast_recv.at[i, n, d], sibling)

        far(final_part(i, n, w, 1 - h), 1).wait_recv()
        far(final_part(i, n, 1 - w, h), 2).wait_send()
        far(final_part(i, n, 1 - w, 1 - h), 2).wait_recv()
        local, sends = extra_copies(i, n)

        @pl.when(bh == shared)
        def _():
            local.wait()
            for src, part, dev, one, two in sends:
                rc(src, part, one, two, dev).wait_send()

        pl.when(bh == shared_beside)(lambda: far(extra_part(i, n), 5).wait_send())
        pl.when(bh == 2 * w + 1 - h)(lambda: far(extra_part(i, n), 4).wait_recv())
        pl.when(bh == 2 * (1 - w) + 1 - h)(lambda: far(extra_part(i, n), 5).wait_recv())

    def tile_of(ref, jh, jw):
        return ref.at[rows_of(jh * 4, 4, 4), rows_of(jw * 32, 32), :]

    def tile_own(src, dst, n):
        return lc(src.at[mine], tile_of(dst, h, w), r.tile_own.at[n])

    def tiles_start(src, dst, n):
        for j, dev in tile_group:
            rc(src.at[j], tile_of(dst, h, w), r.tile_send.at[n], r.tile_recv.at[n], dev).start()
        tile_own(src, dst, n).start()

    def tiles_wait(src, dst, n):
        three = src.at[0:3]
        rc(three, three, r.tile_send.at[n], r.tile_recv.at[n], sibling).wait()
        tile_own(src, dst, n).wait()

    xg, cg = r.x_grid, r.cot_grid
    tiles_start(r.x_tiles, xg, 0)
    gather_start(0)
    r.param[...] = total(0, mid, r.param_in[...])
    tiles_wait(r.x_tiles, xg, 0)

    def grid_chunk(ref, i):
        v = ref[lax.div(i, 4), rows_of(lax.rem(i, 4) * CHUNK, CHUNK), :]
        return v.astype(F32).reshape(2, CELL, chan)

    fill(r.xa, r.xb, lambda i: grid_chunk(xg, i), chan)

    def pump_loop(i, lo, hi):
        def body(s, _):
            gather_pump(i, s)
            return 0

        lax.fori_loop(lo, hi, body, 0)

    pump_loop(0, 1, nb - 3)
    gather_start(1)
    pump_loop(0, nb - 3, nb - 1)
    gather_start(2)
    gather_pump(0, nb - 1)
    gather_pump(1, 1)
    gather_pump(2, 1)
    gather_pump(1, 2)
    gather_finish(0)

    def first_pump(n):
        pl.when(lax.rem(n, 2) == 0)(lambda: gather_pump(1, 3 + lax.div(n, 2)))
        pl.when(n == 3)(lambda: gather_pump(2, 2))

    conv(r.xa, r.xb, whole[0], r.mid1, first_pump)
    def first_last():
        gather_pump(2, 3)
        gather_pump(1, nb - 1)

    sums = total(
        1,
        mid,
        packed(*moments(r.mid1, mid), mid),
        [lambda: gather_pump(1, nb - 2), first_last],
    )
    prepare(0, sums, mid)

    def hidden(src, n, dst):
        value = activated(src, n, mid)

        def body(i, _):
            put(dst, i, value(i))
            return 0

        loop(CHUNKS, body, 0)

    hidden(r.mid1, 0, r.v1)
    gather_pump(2, 4)
    gather_finish(1)
    stats = temporal(0, r.v1, whole[1], r.time1, [lambda: gather_pump(2, 5)])

    def sixth():
        gather_pump(2, 6)

    sums = total(2, chan, packed(*stats, chan), [lambda: gather_start(3), sixth])
    prepare(1, sums, chan)
    fill(r.aa, r.ab, activated(r.time1, 1, chan), chan)
    gather_pump(3, 1)
    gather_pump(2, nb - 1)
    gather_pump(3, 2)
    gather_finish(2)
    tiles_start(r.cot_tiles, cg, 1)

    def second_pump(n):
        pl.when(n < nb - 3)(lambda: gather_pump(3, 3 + n))

    conv(r.aa, r.ab, whole[2], r.mid2, second_pump)
    sums = total(3, mid, packed(*moments(r.mid2, mid), mid), [lambda: gather_finish(3)])
    prepare(2, sums, mid)
    hidden(r.mid2, 2, r.v2)
    stats = temporal(1, r.v2, whole[3], r.time2)
    shared_xq2 = share_x(0, r.aa, r.xq2)
    shared_xq1 = share_x(1, r.xa, r.xq1)
    for i in range(4):
        gather_sent(i)
    share_v2 = share(4, r.v2, r.sib_v)
    sums = total(4, chan, packed(*stats, chan), [lambda: tiles_wait(r.cot_tiles, cg, 1)])
    prepare(3, sums, chan)

    out_grid = r.out_grid

    def grid_put(ref, i, v):
        ref[lax.div(i, 4), rows_of(lax.rem(i, 4) * CHUNK, CHUNK), :] = v.reshape(CHUNK, chan).astype(ref.dtype)

    def slope(y, s):
        return s * (1.0 + y * (1.0 - s))

    def pre_body(i, carry):
        scale, shift, inv, offset = tiles(3, chan)
        v = chunk(r.time2, i)
        y = v * scale + shift + chunk(r.xa, i, MAIN)
        s = sigmoid(y)
        m = keep(i)
        grid_put(out_grid, i, y * s * m)
        d = grid_chunk(cg, i) * m * slope(y, s)
        put(r.grad_pre, i, d)
        t = d * (v * inv - offset)
        return (carry[0] + d[0] + d[1], carry[1] + t[0] + t[1])

    zero_out = jnp.zeros((CELL, chan), F32)
    zero_mid = jnp.zeros((CELL, mid), F32)
    out_grid[HGT] = jnp.zeros((8 * CELL, chan), BF16)
    gg = loop(CHUNKS, pre_body, (zero_out, zero_out))

    def send_tiles(src, dst, n):
        for j, dev in tile_group:
            jh, jw = at_group(j)
            rc(tile_of(src, jh, jw), dst.at[mine], r.tile_send.at[n], r.tile_recv.at[n], dev).start()
        lc(tile_of(src, h, w), dst.at[mine], r.tile_own.at[n]).start()

    def sent_tiles(src, dst, n):
        three = dst.at[0:3]
        rc(three, three, r.tile_send.at[n], r.tile_recv.at[n], sibling).wait()
        lc(tile_of(src, h, w), dst.at[mine], r.tile_own.at[n]).wait()

    send_tiles(out_grid, r.block_out, 2)

    def norm_back(n, sums, width):
        r.norm_part[0, 2 * n : 2 * n + 1, 0:width] = sums[1:2]
        r.norm_part[0, 2 * n + 1 : 2 * n + 2, 0:width] = sums[0:1]
        back = r.back
        back[0, :, 0:width] = jnp.broadcast_to(sums[0:1] / cell_count, (CELL, width))
        back[1, :, 0:width] = jnp.broadcast_to(sums[1:2] / cell_count, (CELL, width))

    def through_norm(n, src, grad, i, width):
        scale, _, inv, offset = tiles(n, width)
        xhat = chunk(src, i) * inv - offset
        bias_part = r.back[0, :, 0:width][None]
        gain_part = r.back[1, :, 0:width][None]
        return scale * (chunk(grad, i, 0, width) - bias_part - xhat * gain_part) * keep(i)

    def through_act(n, src, grad, width):
        def body(i, carry):
            scale, shift, inv, offset = tiles(n, width)
            v = chunk(src, i)
            y = v * scale + shift
            s = sigmoid(y)
            d = chunk(grad, i, 0, width) * keep(i) * slope(y, s)
            put(grad, i, d, 0, width)
            t = d * (v * inv - offset)
            return (carry[0] + d[0] + d[1], carry[1] + t[0] + t[1])

        zero = jnp.zeros((CELL, width), F32)
        return loop(CHUNKS, body, (zero, zero))

    def to_frames(n, src, grad):
        def body(i, _):
            e = through_norm(n, src, grad, i, chan).astype(BF16)
            ef = e.astype(F32)
            put_e(1, i, e.reshape(CHUNK, chan))
            put_lanes(r.down, rows_of(i * CHUNK + CELL, CHUNK, CELL), ef.reshape(CHUNK, chan))
            put_lanes(r.up, rows_of(i * CHUNK, CHUNK), (ef * r.gate[...][None]).reshape(CHUNK, chan))
            return 0

        loop(CHUNKS, body, 0)

    near, far = r.xt, r.xt2

    def spread():
        shared_xq2.wait()
        spread_x(r.xq2)
        shared_xq1.wait()
        spread_x(r.xq1)

    sums = total(5, chan, packed(*gg, chan), [spread, lambda: transposes(r.aa, r.ab, r.xq2, near, far)])
    norm_back(3, sums, chan)
    to_frames(3, r.time2, r.grad_pre)
    shared_e3 = temporal_back(2, whole[3])
    credit(1)
    gg = through_act(2, r.mid2, r.grad_mid, mid)
    shared_e3.wait()
    share_v2.wait()
    def temporal_grads(i, v):
        def first():
            transpose_v(v, r.sib_v)
            temporal_grad(i, 0, 2)

        return [first, lambda: temporal_grad(i, 2, 1)]

    sums = total(6, mid, packed(*gg, mid), temporal_grads(3, r.v2))
    reduce_start(3, 0)
    norm_back(2, sums, mid)

    def fill_e(n, src):
        def value(i):
            v = through_norm(n, src, r.grad_mid, i, mid)
            for part, (c0, cw) in zip(e_all, halves):
                put(part, i, v[:, :, c0 : c0 + cw])
            return v

        fill(r.ea, r.eb, value, mid)

    fill_e(2, r.mid2)
    share_e(0)
    conv_back(r.ea, r.eb, whole[2], r.grad_mid)
    gg = through_act(1, r.time1, r.grad_mid, chan)

    def first_half():
        share_e_wait(0, 0)
        spatial_half(2, near, far, 0)

    sums = total(7, chan, packed(*gg, chan), [lambda: share_e_on(0, 0), first_half])
    reduce_start(2, 0)
    share_v1 = share(5, r.v1, r.sib_v)
    norm_back(1, sums, chan)
    to_frames(1, r.time1, r.grad_mid)
    reduce_middle(3, 0)
    share_e_on(0, 1)

    def second_half():
        share_e_wait(0, 1)
        spatial_half(2, near, far, 1)
        credit(2)
        reduce_start(2, 1)

    shared_e3 = temporal_back(3, whole[1], [second_half])
    credit(0)
    reduce_middle(2, 0)
    gg = through_act(0, r.mid1, r.grad_mid, mid)
    shared_e3.wait()
    share_v1.wait()
    sums = total(8, mid, packed(*gg, mid), temporal_grads(1, r.v1))
    reduce_start(1, 0)
    reduce_middle(2, 1)
    norm_back(0, sums, mid)
    fill_e(0, r.mid1)
    credited(2)
    share_e(1)
    reduce_last(3, 0)
    transposes(r.xa, r.xb, r.xq1, near, far)
    share_e_on(1, 0)
    reduce_out(3)
    sent_tiles(out_grid, r.block_out, 2)
    share_e_wait(1, 0)
    spatial_half(0, near, far, 0)
    reduce_start(0, 0)
    reduce_middle(1, 0)

    def pass_on(k):
        pl.when(k == 2)(lambda: share_e_on(1, 1))

    conv_back(r.ea, r.eb, whole[0], r.grad_mid, pass_on)
    share_e_wait(1, 1)
    spatial_half(0, near, far, 1)
    reduce_start(0, 1)
    reduce_middle(0, 0)

    norm_copy = rc(r.norm_part.at[0], r.norm_part.at[1], r.norm_sem.at[0], r.norm_sem.at[1], beside)
    norm_copy.start()

    def last_body(i, _):
        grid_put(out_grid, i, (chunk(r.grad_mid, i, 0, chan) + chunk(r.grad_pre, i)) * keep(i))
        return 0

    loop(CHUNKS, last_body, 0)
    send_tiles(out_grid, r.grad_input, 3)
    for n in (0, 1):
        reduce_last(2, n)
    reduce_last(1, 0)
    for n in (0, 1):
        final_on(2, n)
    reduce_out(1)
    reduce_last(0, 0)
    norm_copy.wait()
    r.norm_grads[...] = r.norm_part[0] + r.norm_part[1]
    reduce_middle(0, 1)
    final_on(0, 0)
    sent_tiles(out_grid, r.grad_input, 3)
    for n in (0, 1):
        reduce_wait(2, n)
    reduce_wait(3, 0)
    reduce_wait(1, 0)
    reduce_last(0, 1)
    final_on(0, 1)
    for n in (0, 1):
        reduce_wait(0, n)


def per_device_fast(nb, *args):
    (
        inputs,
        starts,
        first_spatial,
        first_mid_gain,
        first_mid_bias,
        first_temporal,
        first_out_gain,
        first_out_bias,
        second_spatial,
        second_mid_gain,
        second_mid_bias,
        second_temporal,
        second_out_gain,
        second_out_bias,
        cotangent,
    ) = args
    micro, frames, side, _, chan = inputs.shape
    mid = first_spatial.shape[1]
    spat, temp = first_spatial.shape[0], first_temporal.shape[0]
    h, w, b = (lax.axis_index(name) for name in ("ha", "wa", "batch"))
    few = frames // 2
    offsets = jnp.arange(side)
    valid = (h * side + offsets < HGT)[:, None] & (w * side + offsets < HGT)[None, :]

    def tiles(array):
        array = array * valid.astype(BF16)[None, None, :, :, None]
        array = array.reshape(micro, 2, few, side, side, chan).transpose(0, 1, 3, 4, 2, 5)
        return array.reshape(4, side, side * few, chan)

    def untiled(array):
        array = array.reshape(micro, 2, side, side, few, chan).transpose(0, 1, 4, 2, 3, 5)
        return array.reshape(micro, frames, side, side, chan).astype(F32)

    gate = (1 - lax.dynamic_slice(starts, (w, h * few), (1, few))).astype(F32)
    gate = jnp.broadcast_to(gate.reshape(few, 1), (few, chan))
    here = jnp.where(h == 0, 1.0, 0.0)

    def placed(shard):
        row = jnp.zeros((mid,), F32)
        return lax.dynamic_update_slice(row, shard.astype(F32) * here, (b * shard.shape[0],))

    param = jnp.stack(
        [
            placed(v)
            for v in (
                first_mid_gain,
                first_mid_bias,
                first_out_gain,
                first_out_bias,
                second_mid_gain,
                second_mid_bias,
                second_out_gain,
                second_out_bias,
            )
        ]
    )
    half = chan // 2
    few_rows = ROWS // CELL

    inputs_of = dict(
        x_tiles=(tiles(inputs), pl.ANY),
        cot_tiles=(tiles(cotangent), pl.ANY),
        gate=(gate, pltpu.VMEM),
        param_in=(param, pltpu.VMEM),
        first_spatial=(first_spatial, pl.ANY),
        first_temporal=(first_temporal, pl.ANY),
        second_spatial=(second_spatial, pl.ANY),
        second_temporal=(second_temporal, pl.ANY),
    )
    outputs_of = dict(
        block_out=((4, side, side * CELL, chan), BF16, pl.ANY),
        grad_input=((4, side, side * CELL, chan), BF16, pl.ANY),
        norm_grads=((8, mid), F32, pltpu.VMEM),
        out1s0=((spat, 512), BF16, pl.ANY),
        out1s1=((spat, mid - 512), BF16, pl.ANY),
        out1t=((2, temp, half), BF16, pl.ANY),
        out2s0=((spat, 512), BF16, pl.ANY),
        out2s1=((spat, mid - 512), BF16, pl.ANY),
        out2t=((2, temp, half), BF16, pl.ANY),
    )
    dma = pltpu.SemaphoreType.DMA
    scratch_of = dict(
        w1s0=pltpu.VMEM((9 * chan, 512), BF16),
        w1s1=pltpu.VMEM((9 * chan, mid - 512), BF16),
        w1t0=pltpu.VMEM((3 * mid, half), BF16),
        w1t1=pltpu.VMEM((3 * mid, half), BF16),
        w2s0=pltpu.VMEM((9 * chan, 512), BF16),
        w2s1=pltpu.VMEM((9 * chan, mid - 512), BF16),
        w2t0=pltpu.VMEM((3 * mid, half), BF16),
        w2t1=pltpu.VMEM((3 * mid, half), BF16),
        x_grid=pltpu.VMEM((8, 8 * CELL, chan), BF16),
        cot_grid=pltpu.VMEM((8, 8 * CELL, chan), BF16),
        out_grid=pltpu.VMEM((8, 8 * CELL, chan), BF16),
        xa=pltpu.VMEM((PADDED, chan), BF16),
        xb=pltpu.VMEM((PADDED, chan), BF16),
        aa=pltpu.VMEM((PADDED, chan), BF16),
        ab=pltpu.VMEM((PADDED, chan), BF16),
        ea=pltpu.VMEM((PADDED, mid), BF16),
        eb=pltpu.VMEM((PADDED, mid), BF16),
        mid1=pltpu.VMEM((ROWS, mid), F32),
        mid2=pltpu.VMEM((ROWS, mid), F32),
        grad_mid=pltpu.VMEM((ROWS, mid), F32),
        v1=pltpu.VMEM((ROWS, mid), BF16),
        v2=pltpu.VMEM((ROWS, mid), BF16),
        time1=pltpu.VMEM((ROWS, chan), F32),
        time2=pltpu.VMEM((ROWS, chan), F32),
        grad_pre=pltpu.VMEM((ROWS, chan), F32),
        down=pltpu.VMEM((chan // 128, ROWS + CHUNK, 128), F32),
        up=pltpu.VMEM((chan // 128, ROWS + CHUNK, 128), F32),
        e3=pltpu.VMEM((2, 3, ROWS, half), BF16),
        sib_e3=pltpu.VMEM((3, ROWS, half), BF16),
        halo_out=pltpu.VMEM((2, few_rows, chan), F32),
        halo_in=pltpu.VMEM((4, 2, few_rows, chan), F32),
        param=pltpu.VMEM((8, mid), F32),
        tile_mid=pltpu.VMEM((2, 4, CELL, mid), F32),
        tile_out=pltpu.VMEM((2, 4, CELL, chan), F32),
        back=pltpu.VMEM((2, CELL, mid), F32),
        norm_part=pltpu.VMEM((2, 8, mid), F32),
        sum_b=pltpu.VMEM((2, 4, 8, mid), F32),
        sum_c=pltpu.VMEM((2, nb // 2, 8, mid), F32),
        own_sem=dma((4, 2)),
        ring_send=dma((4, 2)),
        ring_recv=dma((4, 2, 2, nb)),
        sib_send=dma((4, 2)),
        sib_recv=dma((4, 2)),
        over_send=dma((4, 2)),
        over_recv=dma((4, 2, nb)),
        norm_sem=dma((2,)),
        credit=pltpu.SemaphoreType.REGULAR((3,)),
        sb_send=dma((9,)),
        sb_recv=dma((9,)),
        sc_send=dma((9,)),
        sc_recv=dma((9,)),
        halo_send=dma((4, 2)),
        halo_recv=dma((4, 2)),
        share_send=dma((6,)),
        share_recv=dma((6,)),
        e_all0=pltpu.VMEM((4 * ROWS, 512), BF16),
        e_all1=pltpu.VMEM((4 * ROWS, mid - 512), BF16),
        xq1=pltpu.VMEM((3, 2, PADDED, chan // 4), BF16),
        xq2=pltpu.VMEM((3, 2, PADDED, chan // 4), BF16),
        xt=pltpu.VMEM((mid, 2 * ROWS), BF16),
        xt2=pltpu.VMEM((mid, 2 * ROWS), BF16),
        sib_v=pltpu.VMEM((ROWS, mid), BF16),
        e_send=dma((2, 2)),
        e_recv=dma((2, 2, 2)),
        xq_send=dma((2,)),
        xq_recv=dma((2,)),
        y_send=dma((4, 2)),
        y_recv=dma((4, 2)),
        z_send=dma((4, 2)),
        z_recv=dma((4, 2)),
        cast_send=dma((4, 2, 6)),
        cast_recv=dma((4, 2, 8)),
        out_sem=dma((4, 2, 2)),
        fin_send=dma((4,)),
        fin_recv=dma((4,)),
        tile_send=dma((4,)),
        tile_recv=dma((4,)),
        tile_own=dma((4,)),
    )
    names = (*inputs_of, *outputs_of, *scratch_of)
    cell_count = float(frames * nb * HGT * HGT)
    results = pl.pallas_call(
        functools.partial(block_kernel, (nb, chan, mid, cell_count), names),
        out_shape=[jax.ShapeDtypeStruct(shape, dtype) for shape, dtype, _ in outputs_of.values()],
        in_specs=[pl.BlockSpec(memory_space=space) for _, space in inputs_of.values()],
        out_specs=[pl.BlockSpec(memory_space=space) for _, _, space in outputs_of.values()],
        scratch_shapes=list(scratch_of.values()),
        compiler_params=pltpu.CompilerParams(
            collective_id=0, has_side_effects=True, vmem_limit_bytes=VMEM_LIMIT
        ),
    )(*(array for array, _ in inputs_of.values()))
    got = SimpleNamespace(**dict(zip(outputs_of, results)))

    def spatial(left, right):
        return jnp.concatenate([left, right], axis=1).astype(F32)

    def temporal(pair):
        return jnp.concatenate([pair[0], pair[1]], axis=1).astype(F32)

    def norm(row, like):
        size = like.shape[0]
        return lax.dynamic_slice_in_dim(got.norm_grads[row], b * size, size)

    return (
        untiled(got.block_out),
        untiled(got.grad_input),
        spatial(got.out1s0, got.out1s1),
        norm(0, first_mid_gain),
        norm(1, first_mid_bias),
        temporal(got.out1t),
        norm(2, first_out_gain),
        norm(3, first_out_bias),
        spatial(got.out2s0, got.out2s1),
        norm(4, second_mid_gain),
        norm(5, second_mid_bias),
        temporal(got.out2t),
        norm(6, second_out_gain),
        norm(7, second_out_bias),
    )


def extended(shard, sides, width):
    for axis, dim in sides:
        count, length = (lax.axis_size(axis), shard.shape[dim])
        up = [(i, (i + 1) % count) for i in range(count - 1)]
        down = [(j, i) for i, j in up]
        last = lax.slice_in_dim(shard, length - width, length, axis=dim)
        leading = lax.slice_in_dim(shard, 0, width, axis=dim)
        before = lax.ppermute(last, axis, up)
        after = lax.ppermute(leading, axis, down)
        shard = jnp.concatenate([before, shard, after], axis=dim)
    return shard


def passed_along(shard, axis, by):
    count = lax.axis_size(axis)
    pairs = [(i, i + by) for i in range(count) if 0 <= i + by < count]
    return lax.ppermute(shard, axis, pairs)


def for_sending(shard):

    def short(part):
        return part.astype(jnp.bfloat16) if part.dtype == jnp.float32 else part

    return jax.tree.map(short, shard)


def silu_slope(values):
    sigma = jax.nn.sigmoid(values)
    return sigma * (1.0 + values * (1.0 - sigma))


def spatial_forward(field_in, kernel):
    frames, tile_side = (field_in.shape[0], field_in.shape[1])
    padded = extended(field_in, (("ha", 1), ("wa", 2)), 1)
    pieces = [
        padded[:, offset // 3 : offset // 3 + tile_side, offset % 3 : offset % 3 + tile_side, :]
        for offset in range(9)
    ]
    patches = jnp.concatenate(pieces, axis=-1).reshape(frames * tile_side * tile_side, -1)
    return (patches, jnp.dot(patches, kernel, preferred_element_type=jnp.float32))


def spatial_backward(grad_out, patches, kernel):
    frames, tile_side, channels = (grad_out.shape[0], grad_out.shape[1], grad_out.shape[3])
    row_count = frames * tile_side * tile_side
    padded = extended(grad_out, (("ha", 1), ("wa", 2)), 1)
    pieces = [
        padded[
            :,
            2 - offset // 3 : 2 - offset // 3 + tile_side,
            2 - offset % 3 : 2 - offset % 3 + tile_side,
            :,
        ]
        for offset in range(9)
    ]
    stacked = jnp.concatenate(pieces, axis=-1).reshape(row_count, 9, channels)
    grad_in = jnp.einsum(
        "rkm,kcm->rc", stacked, kernel.reshape(9, -1, channels), preferred_element_type=jnp.float32
    )
    grad_kernel = jnp.einsum(
        "rk,rm->km",
        patches,
        grad_out.reshape(row_count, channels),
        preferred_element_type=jnp.float32,
    )
    return (grad_in, grad_kernel)


def temporal_forward(field_in, clip_gate, kernel):
    frames, tile_side = (field_in.shape[0], field_in.shape[1])
    gated_in = field_in * clip_gate
    earlier = passed_along(field_in[-1:], "batch", 1)
    later_frame = passed_along(gated_in[:1], "batch", -1)
    before = jnp.concatenate([earlier, field_in[:-1]], axis=0) * clip_gate
    after_tap = jnp.concatenate([gated_in[1:], later_frame], axis=0)
    joined = jnp.concatenate([before, field_in, after_tap], axis=-1).reshape(
        frames * tile_side * tile_side, -1
    )
    return (joined, jnp.dot(joined, kernel, preferred_element_type=jnp.float32))


def temporal_backward(grad_out, joined, clip_gate, kernel):
    frames, tile_side, channels = (grad_out.shape[0], grad_out.shape[1], grad_out.shape[3])
    row_count = frames * tile_side * tile_side
    gated_grad = grad_out * clip_gate
    later_frame = passed_along(gated_grad[:1], "batch", -1)
    earlier = passed_along(grad_out[-1:], "batch", 1)
    from_later = jnp.concatenate([gated_grad[1:], later_frame], axis=0)
    from_earlier = jnp.concatenate([earlier, grad_out[:-1]], axis=0) * clip_gate
    stacked = jnp.concatenate([from_later, grad_out, from_earlier], axis=-1).reshape(
        row_count, 3, channels
    )
    grad_in = jnp.einsum(
        "rkc,kmc->rm", stacked, kernel.reshape(3, -1, channels), preferred_element_type=jnp.float32
    )
    grad_kernel = jnp.einsum(
        "rk,rc->kc",
        joined,
        grad_out.reshape(row_count, channels),
        preferred_element_type=jnp.float32,
    )
    return (grad_in, grad_kernel)


def norm_forward(pre_norm, norm_gain, norm_bias, valid_rows, cell_count):
    first_sum = jnp.sum(pre_norm * valid_rows, axis=0)
    square_sum = jnp.sum(pre_norm * pre_norm * valid_rows, axis=0)
    first_sum, square_sum = lax.psum((first_sum, square_sum), ("ha", "wa", "batch"))
    mean_val = first_sum / cell_count
    inv_std = lax.rsqrt(square_sum / cell_count - mean_val * mean_val + epsilon)
    normed = (pre_norm - mean_val) * inv_std
    return (normed, inv_std, normed * norm_gain.astype(jnp.float32) + norm_bias.astype(jnp.float32))


def norm_backward(grad_norm, normed, inv_std, norm_gain, valid_rows, cell_count):
    bias_grad = jnp.sum(grad_norm, axis=0)
    gain_grad = jnp.sum(grad_norm * normed, axis=0)
    bias_grad, gain_grad = lax.psum((bias_grad, gain_grad), ("ha", "wa", "batch"))
    grad_in = (
        valid_rows
        * norm_gain.astype(jnp.float32)
        * inv_std
        * (grad_norm - bias_grad / cell_count - normed * gain_grad / cell_count)
    )
    return (grad_in, gain_grad, bias_grad)


def forward_pair(field_in, weights, clip_gate, valid_rows, cell_count):
    frames, tile_side = (field_in.shape[0], field_in.shape[1])
    patches, spatial_out = spatial_forward(field_in, weights[0])
    mid_hat, mid_scale, mid_norm = norm_forward(
        spatial_out, weights[1], weights[2], valid_rows, cell_count
    )
    hidden = (
        (jax.nn.silu(mid_norm) * valid_rows)
        .astype(jnp.bfloat16)
        .reshape(frames, tile_side, tile_side, -1)
    )
    joined, temporal_out = temporal_forward(hidden, clip_gate, weights[3])
    out_hat, out_scale, out_norm = norm_forward(
        temporal_out, weights[4], weights[5], valid_rows, cell_count
    )
    return ((patches, mid_hat, mid_scale, mid_norm, joined, out_hat, out_scale), out_norm)


def backward_pair(grad_norm, kept, weights, clip_gate, valid_rows, cell_count, tile_side):
    patches, mid_hat, mid_scale, mid_norm, joined, out_hat, out_scale = kept
    frames = clip_gate.shape[0]
    grad_time, out_gain_grad, out_bias_grad = norm_backward(
        grad_norm, out_hat, out_scale, weights[4], valid_rows, cell_count
    )
    grad_time = grad_time.astype(jnp.bfloat16).reshape(frames, tile_side, tile_side, -1)
    grad_hidden, temporal_grad = temporal_backward(grad_time, joined, clip_gate, weights[3])
    grad_mid = grad_hidden * valid_rows * silu_slope(mid_norm)
    grad_spatial, mid_gain_grad, mid_bias_grad = norm_backward(
        grad_mid, mid_hat, mid_scale, weights[1], valid_rows, cell_count
    )
    grad_spatial = grad_spatial.astype(jnp.bfloat16).reshape(frames, tile_side, tile_side, -1)
    grad_in, spatial_grad = spatial_backward(grad_spatial, patches, weights[0])
    return (
        grad_in,
        (spatial_grad, mid_gain_grad, mid_bias_grad, temporal_grad, out_gain_grad, out_bias_grad),
    )


def per_device(
    inputs,
    starts,
    first_spatial,
    first_mid_gain,
    first_mid_bias,
    first_temporal,
    first_out_gain,
    first_out_bias,
    second_spatial,
    second_mid_gain,
    second_mid_bias,
    second_temporal,
    second_out_gain,
    second_out_bias,
    cotangent,
):
    shards = (
        first_spatial,
        first_mid_gain,
        first_mid_bias,
        first_temporal,
        first_out_gain,
        first_out_bias,
        second_spatial,
        second_mid_gain,
        second_mid_bias,
        second_temporal,
        second_out_gain,
        second_out_bias,
    )
    micro_total, frames, tile_side, channels = (
        inputs.shape[0],
        inputs.shape[1],
        inputs.shape[2],
        inputs.shape[4],
    )
    row_count = frames * tile_side * tile_side
    cell_count = frames * lax.axis_size("batch") * HGT * HGT
    offsets = jnp.arange(tile_side)
    inside_h = lax.axis_index("ha") * tile_side + offsets < HGT
    inside_w = lax.axis_index("wa") * tile_side + offsets < HGT
    valid_grid = inside_h[:, None] & inside_w[None, :]
    valid_tile = valid_grid.astype(jnp.bfloat16)[None, :, :, None]
    valid_rows = jnp.broadcast_to(
        valid_grid.astype(jnp.float32)[None], (frames, tile_side, tile_side)
    ).reshape(row_count, 1)
    results = []
    input_grads = []
    kernel_total = None
    norm_total = None
    for micro_step in range(micro_total):
        gathered = (
            lax.all_gather(shards[0], "batch", axis=0, tiled=True),
            lax.all_gather(shards[1], "batch", axis=0, tiled=True),
            lax.all_gather(shards[2], "batch", axis=0, tiled=True),
            lax.all_gather(shards[3], "batch", axis=0, tiled=True),
            lax.all_gather(shards[4], "batch", axis=0, tiled=True),
            lax.all_gather(shards[5], "batch", axis=0, tiled=True),
            lax.all_gather(shards[6], "batch", axis=0, tiled=True),
            lax.all_gather(shards[7], "batch", axis=0, tiled=True),
            lax.all_gather(shards[8], "batch", axis=0, tiled=True),
            lax.all_gather(shards[9], "batch", axis=0, tiled=True),
            lax.all_gather(shards[10], "batch", axis=0, tiled=True),
            lax.all_gather(shards[11], "batch", axis=0, tiled=True),
        )
        clip_gate = (1 - starts[micro_step]).astype(jnp.bfloat16).reshape(frames, 1, 1, 1)
        x_in = inputs[micro_step] * valid_tile
        first_kept, first_norm = forward_pair(
            x_in, gathered[0:6], clip_gate, valid_rows, cell_count
        )
        first_act = (
            (jax.nn.silu(first_norm) * valid_rows)
            .astype(jnp.bfloat16)
            .reshape(frames, tile_side, tile_side, channels)
        )
        second_kept, second_norm = forward_pair(
            first_act, gathered[6:12], clip_gate, valid_rows, cell_count
        )
        pre_out = second_norm + x_in.reshape(row_count, channels).astype(jnp.float32)
        results.append(
            (jax.nn.silu(pre_out) * valid_rows).reshape(frames, tile_side, tile_side, channels)
        )
        grad_pre = (
            cotangent[micro_step].reshape(row_count, channels).astype(jnp.float32)
            * valid_rows
            * silu_slope(pre_out)
        )
        grad_act, second_grads = backward_pair(
            grad_pre, second_kept, gathered[6:12], clip_gate, valid_rows, cell_count, tile_side
        )
        grad_first = grad_act * valid_rows * silu_slope(first_norm)
        grad_conv, first_grads = backward_pair(
            grad_first, first_kept, gathered[0:6], clip_gate, valid_rows, cell_count, tile_side
        )
        input_grads.append(
            ((grad_conv + grad_pre) * valid_rows).reshape(frames, tile_side, tile_side, channels)
        )
        step_grads = first_grads + second_grads
        kernel_now = (step_grads[0], step_grads[3], step_grads[6], step_grads[9])
        norm_now = (
            step_grads[1],
            step_grads[2],
            step_grads[4],
            step_grads[5],
            step_grads[7],
            step_grads[8],
            step_grads[10],
            step_grads[11],
        )
        if micro_step == 0:
            kernel_total = kernel_now
            norm_total = norm_now
        else:
            kernel_total = jax.tree.map(jnp.add, kernel_total, kernel_now)
            norm_total = jax.tree.map(jnp.add, norm_total, norm_now)
    kernel_total = lax.psum_scatter(kernel_total, "batch", scatter_dimension=0, tiled=True)
    kernel_total = jax.tree.map(
        lambda part: part.astype(jnp.float32), lax.psum(for_sending(kernel_total), ("ha", "wa"))
    )
    shard_index = lax.axis_index("batch")
    batch_count = lax.axis_size("batch")
    norm_shards = tuple(
        (
            lax.dynamic_slice_in_dim(
                full_sum,
                shard_index * (full_sum.shape[0] // batch_count),
                full_sum.shape[0] // batch_count,
            )
            for full_sum in norm_total
        )
    )
    return (
        jnp.stack(results),
        jnp.stack(input_grads),
        kernel_total[0],
        norm_shards[0],
        norm_shards[1],
        kernel_total[1],
        norm_shards[2],
        norm_shards[3],
        kernel_total[2],
        norm_shards[4],
        norm_shards[5],
        kernel_total[3],
        norm_shards[6],
        norm_shards[7],
    )


def solution(mesh):
    in_specs = (
        P(None, "batch", "ha", "wa", None),
        P(None, "batch"),
        P("batch", None),
        P("batch"),
        P("batch"),
        P("batch", None),
        P("batch"),
        P("batch"),
        P("batch", None),
        P("batch"),
        P("batch"),
        P("batch", None),
        P("batch"),
        P("batch"),
        P(None, "batch", "ha", "wa", None),
    )
    out_specs = (
        P(None, "batch", "ha", "wa", None),
        P(None, "batch", "ha", "wa", None),
        P("batch", None),
        P("batch"),
        P("batch"),
        P("batch", None),
        P("batch"),
        P("batch"),
        P("batch", None),
        P("batch"),
        P("batch"),
        P("batch", None),
        P("batch"),
        P("batch"),
    )
    batch = mesh.shape["batch"]

    def program(*args):
        spat, temp = args[2].shape[0], args[5].shape[0]
        fits = args[0].shape == (2, 16, 4, 4, 512) and args[2].shape[1] == 1152
        if fits and batch == 8 and spat * batch == 9 * 512 and temp * batch == 3 * 1152:
            return per_device_fast(batch, *args)
        return per_device(*args)

    return jax.shard_map(
        program, mesh=mesh, in_specs=in_specs, out_specs=out_specs, check_vma=False
    )
```

profile of v0, /device:TPU:3, one launch (start us, length us, event | category | flops | bytes accessed | tf_op | source)
XLA Modules:
  0.0 357.0 jit_solution(2147944354564909309)
XLA Ops:
  0.8 0.1 and_convert_fusion
  0.8 1.7 broadcast_multiply_fusion
  2.5 1.1 copy.29
  3.6 1.1 copy.30
  4.7 0.1 convert_bitcast_fusion.2
  4.8 0.7 broadcast_in_dim.5.all_refs_2_
  5.5 0.2 dynamic_update_slice.32
  5.7 0.2 dynamic_update_slice.33
  5.9 0.2 dynamic_update_slice.34
  6.1 0.2 dynamic_update_slice.35
  6.3 0.2 dynamic_update_slice.36
  6.5 0.2 dynamic_update_slice.37
  6.7 0.2 dynamic_update_slice.38
  6.9 0.2 dynamic_update_slice.39
  7.1 0.7 stack.38.all_refs_3_
  7.7 334.1 %shard_map.254 = (bf16[4,4,32,512]{3,2,1,0:T(8,128)(2,1)}, bf16[4,4,32,512]{3,2,1,0:T(8,128)(2,1)}, f32[8,1152]{1,0:T(8,128)}, bf16[576,512]{1,0:T(8,128)(2,1)},...) custom-call(bf16[4,4,32,512]{3,2,1,0:T(8,128)(2,1)} %bitcast.54, ...), custom_call_target="tpu_custom_call" | custom-call | tf_op jit(solution)/shard_map/pallas_call | solution.py:1291
  341.9 1.2 convert_bitcast_fusion.1
  343.1 1.6 copy.31
  344.8 0.1 convert_bitcast_fusion
  344.9 1.6 copy.32
  346.6 1.7 maximum_convert_fusion
  348.3 0.6 constant_dynamic-slice_fusion.7
  348.9 0.6 constant_dynamic-slice_fusion.6
  349.6 1.0 maximum_convert_fusion.2
  350.6 0.6 fusion
  351.2 0.6 fusion.1
  351.8 1.7 maximum_convert_fusion.1
  353.5 0.6 constant_dynamic-slice_fusion.3
  354.1 0.6 constant_dynamic-slice_fusion.2
  354.8 1.0 maximum_convert_fusion.3
  355.8 0.6 fusion.2
  356.4 0.6 fusion.3
  (50 shorter events, 0.2 us)
Async XLA Ops:
  0.6 4.1 %copy-start.16 = (s32[2,16]{1,0:T(2,128)S(1)}, s32[2,16]{1,0:T(2,128)}, u32[]{:S(2)}) copy-start(s32[2,16]{1,0:T(2,128)} %param.16) | copy-start | bytes 388
  0.7 4.8 %copy-start.8 = (bf16[144]{0:T(256)(128)(2,1)S(1)}, bf16[144]{0:T(256)(128)(2,1)}, u32[]{:S(2)}) copy-start(bf16[144]{0:T(256)(128)(2,1)} %param.19) | copy-start | bytes 868
  0.7 4.8 %copy-start.9 = (bf16[144]{0:T(256)(128)(2,1)S(1)}, bf16[144]{0:T(256)(128)(2,1)}, u32[]{:S(2)}) copy-start(bf16[144]{0:T(256)(128)(2,1)} %param.18) | copy-start | bytes 868
  0.7 5.2 %copy-start.10 = (bf16[64]{0:T(256)(128)(2,1)S(1)}, bf16[64]{0:T(256)(128)(2,1)}, u32[]{:S(2)}) copy-start(bf16[64]{0:T(256)(128)(2,1)} %param.22) | copy-start | bytes 388
  0.7 5.2 %copy-start.11 = (bf16[64]{0:T(256)(128)(2,1)S(1)}, bf16[64]{0:T(256)(128)(2,1)}, u32[]{:S(2)}) copy-start(bf16[64]{0:T(256)(128)(2,1)} %param.21) | copy-start | bytes 388
  0.7 5.6 %copy-start.12 = (bf16[144]{0:T(256)(128)(2,1)S(1)}, bf16[144]{0:T(256)(128)(2,1)}, u32[]{:S(2)}) copy-start(bf16[144]{0:T(256)(128)(2,1)} %param.25) | copy-start | bytes 868
  0.7 5.6 %copy-start.13 = (bf16[144]{0:T(256)(128)(2,1)S(1)}, bf16[144]{0:T(256)(128)(2,1)}, u32[]{:S(2)}) copy-start(bf16[144]{0:T(256)(128)(2,1)} %param.24) | copy-start | bytes 868
  0.7 5.9 %copy-start.14 = (bf16[64]{0:T(256)(128)(2,1)S(1)}, bf16[64]{0:T(256)(128)(2,1)}, u32[]{:S(2)}) copy-start(bf16[64]{0:T(256)(128)(2,1)} %param.28) | copy-start | bytes 388
  0.7 5.9 %copy-start.15 = (bf16[64]{0:T(256)(128)(2,1)S(1)}, bf16[64]{0:T(256)(128)(2,1)}, u32[]{:S(2)}) copy-start(bf16[64]{0:T(256)(128)(2,1)} %param.27) | copy-start | bytes 388
  341.9 2.9 copy-start.4
  343.1 3.5 copy-start.1
  343.1 3.5 copy-start.3
  344.9 3.4 copy-start.7
  344.9 4.7 %copy-start.6 = (bf16[2,432,256]{2,1,0:T(8,128)(2,1)S(1)}, bf16[2,432,256]{2,1,0:T(8,128)(2,1)}, u32[]{:S(2)}) copy-start(bf16[2,432,256]{2,1,0:T(8,128)(2,1)} %get-tuple-element.28) | copy-start | bytes 1327108
  346.6 5.2 %copy-start = (bf16[576,640]{1,0:T(8,128)(2,1)S(1)}, bf16[576,640]{1,0:T(8,128)(2,1)}, u32[]{:S(2)}) copy-start(bf16[576,640]{1,0:T(8,128)(2,1)} %get-tuple-element.30) | copy-start | bytes 2211844
  346.6 5.2 %copy-start.2 = (bf16[576,512]{1,0:T(8,128)(2,1)S(1)}, bf16[576,512]{1,0:T(8,128)(2,1)}, u32[]{:S(2)}) copy-start(bf16[576,512]{1,0:T(8,128)(2,1)} %get-tuple-element.29) | copy-start | bytes 1769476
  349.6 5.2 %copy-start.5 = (bf16[2,432,256]{2,1,0:T(8,128)(2,1)S(1)}, bf16[2,432,256]{2,1,0:T(8,128)(2,1)}, u32[]{:S(2)}) copy-start(bf16[2,432,256]{2,1,0:T(8,128)(2,1)} %get-tuple-element.31) | copy-start | bytes 1327108
where the time goes:
time: 359 us; the launch traced here: 357 us
  Pallas kernels  334 us (93%)
  local copies, waits for them, and re-layouts  13.2 us (4%)
  other arithmetic  8.63 us (2%)
    pallas_call x1, Pallas kernels, per_device_fast(): pl.pallas_call(functools.partial(block_kernel, (nb, chan, mid, cell_count...  334 us

commit v1 on v0

--- a/solution.py
+++ b/solution.py
@@ -125,7 +125,9 @@
     shared = 2 * w + h
     shared_beside = 2 * (1 - w) + h
     way = 1 - 2 * h
-    onward = (h, w, at(pos + way))
+    ways = (way, -way)
+    onward = [(h, w, at(pos + d)) for d in ways]
+    steps = (nb // 2, nb // 2 - 1)
     third = temp // 3
 
     def taken(i, core, side):
@@ -148,7 +150,7 @@
 
     def pieces(i):
         start, size = taken(i, h, w)
-        if i:
+        if i % 2:
             return ((start, size),)
         return ((start, size // 2), (start + size // 2, size // 2))
 
@@ -162,62 +164,60 @@
         rows = spat if i % 2 == 0 else temp
         return lc(rows_from(i, c, (0, rows)), rows_in(i, c, b, (0, rows)), r.own_sem.at[i, c])
 
-    def ring(i, c, k, s, owner, from_shard=False):
+    def ring(i, c, k, d, s, owner, from_shard=False):
         part = pieces(i)[k]
         dst = rows_in(i, c, owner, part)
         src = rows_from(i, c, part) if from_shard else dst
-        return rc(src, dst, r.ring_send.at[i, c], r.ring_recv.at[i, c, k, s], onward)
+        return rc(src, dst, r.ring_send.at[i, c], r.ring_recv.at[i, c, k, d, s], onward[d])
 
     def cross(i, c, owner, part):
         ref = rows_in(i, c, owner, part)
         return rc(ref, ref, r.sib_send.at[i, c], r.sib_recv.at[i, c], sibling)
 
-    def over(i, c, s, owner, part):
+    def over(i, c, d, s, owner, part):
         ref = rows_in(i, c, owner, part)
-        return rc(ref, ref, r.over_send.at[i, c], r.over_recv.at[i, c, s], beside)
+        return rc(ref, ref, r.over_send.at[i, c], r.over_recv.at[i, c, d, s], beside)
 
     def gather_start(i):
         for k in range(len(pieces(i))):
-            for c in (0, 1):
-                ring(i, c, k, 1, b, True).start()
+            for d in (0, 1):
+                for c in (0, 1):
+                    ring(i, c, k, d, 1, b, True).start()
         for c in (0, 1):
             own_copy(i, c).start()
 
+    def owners(s):
+        return [(d, at(pos - ways[d] * s)) for d in (0, 1) if s <= steps[d]]
+
     def gather_relay(i, s):
-        owner = at(pos - way * s)
-
         def work():
             part = crosses(i, h, 1 - w)
+            for d, owner in owners(s):
+                for c in (0, 1):
+                    over(i, c, d, s, owner, part).wait_recv()
+                    cross(i, c, owner, part).start()
+
+        crossing(i, work)
+
+    def gather_pump(i, s):
+        for k in range(len(pieces(i))):
+            for d, owner in owners(s):
+                for c in (0, 1):
+                    ring(i, c, k, d, s, owner).wait_recv()
+                    if s < steps[d]:
+                        ring(i, c, k, d, s + 1, owner).start()
+        for d, owner in owners(s):
             for c in (0, 1):
-                over(i, c, s, owner, part).wait_recv()
-                cross(i, c, owner, part).start()
-
-        crossing(i, work)
-
-    def gather_pump(i, s):
-        owner = at(pos - way * s)
-        for k in range(len(pieces(i))):
-            for c in (0, 1):
-                ring(i, c, k, s, owner).wait_recv()
-                if isinstance(s, int):
-                    if s < nb - 1:
-                        ring(i, c, k, s + 1, owner).start()
-                else:
-                    pl.when(s < nb - 1)(lambda k=k, c=c: ring(i, c, k, s + 1, owner).start())
-        for c in (0, 1):
-            crossing(i, lambda c=c: over(i, c, s, owner, crosses(i, h, w)).start())
-            cross(i, c, owner, taken(i, h, w)).start()
-        if isinstance(s, int):
-            if s > 1:
-                gather_relay(i, s - 1)
-        else:
-            pl.when(s > 1)(lambda: gather_relay(i, s - 1))
+                crossing(i, lambda c=c, d=d, owner=owner: over(i, c, d, s, owner, crosses(i, h, w)).start())
+                cross(i, c, owner, taken(i, h, w)).start()
+        if s > 1:
+            gather_relay(i, s - 1)
 
     def span(i, c, size):
         return whole[i][c].at[0 : (nb - 1) * size, :]
 
     def gather_finish(i):
-        gather_relay(i, nb - 1)
+        gather_relay(i, steps[0])
 
         def arrived(size):
             for c in (0, 1):
@@ -848,37 +848,23 @@
 
     fill(r.xa, r.xb, lambda i: grid_chunk(xg, i), chan)
 
-    def pump_loop(i, lo, hi):
-        def body(s, _):
-            gather_pump(i, s)
-            return 0
-
-        lax.fori_loop(lo, hi, body, 0)
-
-    pump_loop(0, 1, nb - 3)
+    last = steps[0]
+    for step in range(1, last):
+        gather_pump(0, step)
     gather_start(1)
-    pump_loop(0, nb - 3, nb - 1)
     gather_start(2)
-    gather_pump(0, nb - 1)
-    gather_pump(1, 1)
-    gather_pump(2, 1)
-    gather_pump(1, 2)
+    gather_pump(0, last)
     gather_finish(0)
 
     def first_pump(n):
-        pl.when(lax.rem(n, 2) == 0)(lambda: gather_pump(1, 3 + lax.div(n, 2)))
-        pl.when(n == 3)(lambda: gather_pump(2, 2))
+        pl.when(n == 0)(lambda: gather_pump(1, 1))
+        pl.when(n == 2)(lambda: gather_pump(1, 2))
+        pl.when(n == 3)(lambda: gather_pump(2, 1))
+        pl.when(n == 5)(lambda: gather_pump(1, 3))
 
     conv(r.xa, r.xb, whole[0], r.mid1, first_pump)
-    def first_last():
-        gather_pump(2, 3)
-        gather_pump(1, nb - 1)
-
     sums = total(
-        1,
-        mid,
-        packed(*moments(r.mid1, mid), mid),
-        [lambda: gather_pump(1, nb - 2), first_last],
+        1, mid, packed(*moments(r.mid1, mid), mid), [lambda: gather_pump(1, last), lambda: gather_pump(2, 2)]
     )
     prepare(0, sums, mid)
 
@@ -892,27 +878,27 @@
         loop(CHUNKS, body, 0)
 
     hidden(r.mid1, 0, r.v1)
-    gather_pump(2, 4)
     gather_finish(1)
-    stats = temporal(0, r.v1, whole[1], r.time1, [lambda: gather_pump(2, 5)])
-
-    def sixth():
-        gather_pump(2, 6)
-
-    sums = total(2, chan, packed(*stats, chan), [lambda: gather_start(3), sixth])
+    stats = temporal(0, r.v1, whole[1], r.time1, [lambda: gather_pump(2, 3)])
+    sums = total(
+        2, chan, packed(*stats, chan), [lambda: gather_start(3), lambda: gather_pump(2, last)]
+    )
     prepare(1, sums, chan)
     fill(r.aa, r.ab, activated(r.time1, 1, chan), chan)
-    gather_pump(3, 1)
-    gather_pump(2, nb - 1)
-    gather_pump(3, 2)
     gather_finish(2)
     tiles_start(r.cot_tiles, cg, 1)
 
     def second_pump(n):
-        pl.when(n < nb - 3)(lambda: gather_pump(3, 3 + n))
+        for step in range(1, last):
+            pl.when(n == 2 * step - 1)(lambda step=step: gather_pump(3, step))
 
     conv(r.aa, r.ab, whole[2], r.mid2, second_pump)
-    sums = total(3, mid, packed(*moments(r.mid2, mid), mid), [lambda: gather_finish(3)])
+
+    def last_piece():
+        gather_pump(3, last)
+        gather_finish(3)
+
+    sums = total(3, mid, packed(*moments(r.mid2, mid), mid), [last_piece])
     prepare(2, sums, mid)
     hidden(r.mid2, 2, r.v2)
     stats = temporal(1, r.v2, whole[3], r.time2)
@@ -1247,11 +1233,11 @@
         sum_c=pltpu.VMEM((2, nb // 2, 8, mid), F32),
         own_sem=dma((4, 2)),
         ring_send=dma((4, 2)),
-        ring_recv=dma((4, 2, 2, nb)),
+        ring_recv=dma((4, 2, 2, 2, nb // 2 + 1)),
         sib_send=dma((4, 2)),
         sib_recv=dma((4, 2)),
         over_send=dma((4, 2)),
-        over_recv=dma((4, 2, nb)),
+        over_recv=dma((4, 2, 2, nb // 2 + 1)),
         norm_sem=dma((2,)),
         credit=pltpu.SemaphoreType.REGULAR((3,)),
         sb_send=dma((9,)),

time: 359 us -> 355 us (0.989)
  no operation moved by 1% of the time
where the time goes in v1:
time: 355 us; the launch traced here: 354 us
  Pallas kernels  331 us (93%)
  local copies, waits for them, and re-layouts  13.2 us (4%)
  other arithmetic  8.63 us (2%)
    pallas_call x1, Pallas kernels, per_device_fast(): pl.pallas_call(functools.partial(block_kernel, (nb, chan, mid, cell_count...  331 us

profile of v1, /device:TPU:3, one launch (start us, length us, event | category | flops | bytes accessed | tf_op | source)
XLA Modules:
  0.0 354.3 jit_solution(7522849085808932914)
XLA Ops:
  0.8 0.1 and_convert_fusion
  0.8 1.7 broadcast_multiply_fusion
  2.5 1.1 copy.29
  3.6 1.1 copy.30
  4.7 0.1 convert_bitcast_fusion.2
  4.8 0.7 broadcast_in_dim.5.all_refs_2_
  5.5 0.2 dynamic_update_slice.32
  5.7 0.2 dynamic_update_slice.33
  5.9 0.2 dynamic_update_slice.34
  6.1 0.2 dynamic_update_slice.35
  6.3 0.2 dynamic_update_slice.36
  6.5 0.2 dynamic_update_slice.37
  6.7 0.2 dynamic_update_slice.38
  6.9 0.2 dynamic_update_slice.39
  7.1 0.7 stack.38.all_refs_3_
  7.7 331.4 %shard_map.254 = (bf16[4,4,32,512]{3,2,1,0:T(8,128)(2,1)}, bf16[4,4,32,512]{3,2,1,0:T(8,128)(2,1)}, f32[8,1152]{1,0:T(8,128)}, bf16[576,512]{1,0:T(8,128)(2,1)},...) custom-call(bf16[4,4,32,512]{3,2,1,0:T(8,128)(2,1)} %bitcast.54, ...), custom_call_target="tpu_custom_call" | custom-call | tf_op jit(solution)/shard_map/pallas_call | solution.py:1277
  339.2 1.2 convert_bitcast_fusion.1
  340.4 1.6 copy.31
  342.1 0.1 convert_bitcast_fusion
  342.2 1.6 copy.32
  343.9 1.7 maximum_convert_fusion
  345.6 0.6 constant_dynamic-slice_fusion.7
  346.3 0.6 constant_dynamic-slice_fusion.6
  346.9 1.0 maximum_convert_fusion.2
  348.0 0.6 fusion
  348.5 0.6 fusion.1
  349.1 1.7 maximum_convert_fusion.1
  350.8 0.6 constant_dynamic-slice_fusion.3
  351.5 0.6 constant_dynamic-slice_fusion.2
  352.1 1.0 maximum_convert_fusion.3
  353.1 0.6 fusion.2
  353.7 0.6 fusion.3
  (50 shorter events, 0.2 us)
Async XLA Ops:
  0.6 4.1 %copy-start.16 = (s32[2,16]{1,0:T(2,128)S(1)}, s32[2,16]{1,0:T(2,128)}, u32[]{:S(2)}) copy-start(s32[2,16]{1,0:T(2,128)} %param.16) | copy-start | bytes 388
  0.7 4.8 %copy-start.8 = (bf16[144]{0:T(256)(128)(2,1)S(1)}, bf16[144]{0:T(256)(128)(2,1)}, u32[]{:S(2)}) copy-start(bf16[144]{0:T(256)(128)(2,1)} %param.19) | copy-start | bytes 868
  0.7 4.8 %copy-start.9 = (bf16[144]{0:T(256)(128)(2,1)S(1)}, bf16[144]{0:T(256)(128)(2,1)}, u32[]{:S(2)}) copy-start(bf16[144]{0:T(256)(128)(2,1)} %param.18) | copy-start | bytes 868
  0.7 5.2 %copy-start.10 = (bf16[64]{0:T(256)(128)(2,1)S(1)}, bf16[64]{0:T(256)(128)(2,1)}, u32[]{:S(2)}) copy-start(bf16[64]{0:T(256)(128)(2,1)} %param.22) | copy-start | bytes 388
  0.7 5.2 %copy-start.11 = (bf16[64]{0:T(256)(128)(2,1)S(1)}, bf16[64]{0:T(256)(128)(2,1)}, u32[]{:S(2)}) copy-start(bf16[64]{0:T(256)(128)(2,1)} %param.21) | copy-start | bytes 388
  0.7 5.6 %copy-start.12 = (bf16[144]{0:T(256)(128)(2,1)S(1)}, bf16[144]{0:T(256)(128)(2,1)}, u32[]{:S(2)}) copy-start(bf16[144]{0:T(256)(128)(2,1)} %param.25) | copy-start | bytes 868
  0.7 5.6 %copy-start.13 = (bf16[144]{0:T(256)(128)(2,1)S(1)}, bf16[144]{0:T(256)(128)(2,1)}, u32[]{:S(2)}) copy-start(bf16[144]{0:T(256)(128)(2,1)} %param.24) | copy-start | bytes 868
  0.7 5.9 %copy-start.14 = (bf16[64]{0:T(256)(128)(2,1)S(1)}, bf16[64]{0:T(256)(128)(2,1)}, u32[]{:S(2)}) copy-start(bf16[64]{0:T(256)(128)(2,1)} %param.28) | copy-start | bytes 388
  0.7 5.9 %copy-start.15 = (bf16[64]{0:T(256)(128)(2,1)S(1)}, bf16[64]{0:T(256)(128)(2,1)}, u32[]{:S(2)}) copy-start(bf16[64]{0:T(256)(128)(2,1)} %param.27) | copy-start | bytes 388
  339.2 2.9 copy-start.4
  340.4 3.5 copy-start.1
  340.4 3.5 copy-start.3
  342.2 3.4 copy-start.7
  342.2 4.7 %copy-start.6 = (bf16[2,432,256]{2,1,0:T(8,128)(2,1)S(1)}, bf16[2,432,256]{2,1,0:T(8,128)(2,1)}, u32[]{:S(2)}) copy-start(bf16[2,432,256]{2,1,0:T(8,128)(2,1)} %get-tuple-element.28) | copy-start | bytes 1327108
  343.9 5.2 %copy-start = (bf16[576,640]{1,0:T(8,128)(2,1)S(1)}, bf16[576,640]{1,0:T(8,128)(2,1)}, u32[]{:S(2)}) copy-start(bf16[576,640]{1,0:T(8,128)(2,1)} %get-tuple-element.30) | copy-start | bytes 2211844
  343.9 5.2 %copy-start.2 = (bf16[576,512]{1,0:T(8,128)(2,1)S(1)}, bf16[576,512]{1,0:T(8,128)(2,1)}, u32[]{:S(2)}) copy-start(bf16[576,512]{1,0:T(8,128)(2,1)} %get-tuple-element.29) | copy-start | bytes 1769476
  346.9 5.2 %copy-start.5 = (bf16[2,432,256]{2,1,0:T(8,128)(2,1)S(1)}, bf16[2,432,256]{2,1,0:T(8,128)(2,1)}, u32[]{:S(2)}) copy-start(bf16[2,432,256]{2,1,0:T(8,128)(2,1)} %get-tuple-element.31) | copy-start | bytes 1327108

commit v2 on v1

--- a/solution.py
+++ b/solution.py
@@ -96,6 +96,12 @@
         q = lax.rem(pos_b + d, 4)
         plane.append((q, (lax.div(q, 2), w, b - par + lax.rem(q, 2))))
     depth = nb // 2
+    place = (h * 2 + par) * depth + bh
+    crowd = []
+    for d in range(1, 2 * nb):
+        q = lax.rem(place + d, 2 * nb)
+        side, far = lax.div(q, depth), lax.rem(q, depth)
+        crowd.append((lax.div(side, 2), w, 2 * far + lax.rem(side, 2)))
     line = []
     for d in range(1, depth):
         q = lax.rem(bh + d, depth)
@@ -112,8 +118,8 @@
     def lc(src, dst, sem):
         return pltpu.make_async_copy(src, dst, sem)
 
-    partners = [sibling, beside, (h, w, at(pos + 1)), (h, w, at(pos - 1)), later_dev, earlier_dev]
-    partners += [dev for _, dev in tile_group + plane + line]
+    partners = []
+    partners += [dev for _, dev in tile_group] + crowd
     barrier = pltpu.get_barrier_semaphore()
     for dev in partners:
         pl.semaphore_signal(barrier, inc=1, device_id=named(dev), device_id_type=MESH)
@@ -248,6 +254,21 @@
 
     def total(k, width, value, works=()):
         slot = k % 2
+        if width == chan:
+            flat, me = r.sum_flat, pos_b * depth + bh
+            flat[slot, me] = value
+            for dev in crowd:
+                part = flat.at[slot, me]
+                rc(part, part, r.sb_send.at[k], r.sb_recv.at[k], dev).start()
+            for work in works:
+                if work:
+                    work()
+            ref = flat.at[slot, 0 : len(crowd)]
+            every = rc(ref, ref, r.sb_send.at[k], r.sb_recv.at[k], sibling)
+            every.wait_recv()
+            result = jnp.sum(flat[slot], axis=0)
+            every.wait_send()
+            return jnp.concatenate([result[2 * n : 2 * n + 2] for n in range(4)], axis=1)
         wide = value.shape[1]
         cols = pl.ds(0, wide)
         works = list(works) + [None] * 2
@@ -397,15 +418,18 @@
 
         lax.fori_loop(0, 3, body, 0)
 
-    def send_frames(k):
+    def send_frames(k, which=(0, 1)):
         down, up = r.down, r.up
         count = ROWS // CELL
-        for c in range(chan // 128):
-            lanes = pl.ds(128 * c, 128)
-            r.halo_out[0, :, lanes] = down[c, pl.ds(2 * CELL - 1, count, stride=CELL), :]
-            r.halo_out[1, :, lanes] = up[c, pl.ds(0, count, stride=CELL), :]
         copies = []
-        for n, dev in ((0, later_dev), (1, earlier_dev)):
+        for n in which:
+            for c in range(chan // 128):
+                lanes = pl.ds(128 * c, 128)
+                if n == 0:
+                    r.halo_out[0, :, lanes] = down[c, pl.ds(2 * CELL - 1, count, stride=CELL), :]
+                else:
+                    r.halo_out[1, :, lanes] = up[c, pl.ds(0, count, stride=CELL), :]
+            dev = (later_dev, earlier_dev)[n]
             copies.append(
                 rc(r.halo_out.at[n], r.halo_in.at[k, n], r.halo_send.at[k, n], r.halo_recv.at[k, n], dev)
             )
@@ -445,10 +469,11 @@
     def temporal(k, v, weight, out, works=()):
         works = list(works) + [None] * 2
         put_lanes(r.down, pl.ds(CELL, ROWS), nn(v[...], both_halves(weight, 0, mid)))
+        copies = send_frames(k, (0,))
         y2 = nn(v[...], both_halves(weight, 2 * mid, mid))
         y2 = (y2.reshape(ROWS // CELL, CELL, chan) * r.gate[...][None]).reshape(ROWS, chan)
         put_lanes(r.up, pl.ds(0, ROWS), y2)
-        copies = send_frames(k)
+        copies += send_frames(k, (1,))
         out[...] = nn(v[...], both_halves(weight, mid, mid))
         if works[0]:
             works[0]()
@@ -849,23 +874,20 @@
     fill(r.xa, r.xb, lambda i: grid_chunk(xg, i), chan)
 
     last = steps[0]
+    gather_start(1)
     for step in range(1, last):
         gather_pump(0, step)
-    gather_start(1)
+        gather_pump(1, step)
     gather_start(2)
     gather_pump(0, last)
+    gather_pump(1, last)
     gather_finish(0)
 
     def first_pump(n):
-        pl.when(n == 0)(lambda: gather_pump(1, 1))
-        pl.when(n == 2)(lambda: gather_pump(1, 2))
-        pl.when(n == 3)(lambda: gather_pump(2, 1))
-        pl.when(n == 5)(lambda: gather_pump(1, 3))
+        pl.when(n == 1)(lambda: gather_pump(2, 1))
 
     conv(r.xa, r.xb, whole[0], r.mid1, first_pump)
-    sums = total(
-        1, mid, packed(*moments(r.mid1, mid), mid), [lambda: gather_pump(1, last), lambda: gather_pump(2, 2)]
-    )
+    sums = total(1, mid, packed(*moments(r.mid1, mid), mid), [lambda: gather_pump(2, 2), lambda: gather_finish(1)])
     prepare(0, sums, mid)
 
     def hidden(src, n, dst):
@@ -878,7 +900,6 @@
         loop(CHUNKS, body, 0)
 
     hidden(r.mid1, 0, r.v1)
-    gather_finish(1)
     stats = temporal(0, r.v1, whole[1], r.time1, [lambda: gather_pump(2, 3)])
     sums = total(
         2, chan, packed(*stats, chan), [lambda: gather_start(3), lambda: gather_pump(2, last)]
@@ -995,10 +1016,10 @@
         shared_xq1.wait()
         spread_x(r.xq1)
 
-    sums = total(5, chan, packed(*gg, chan), [spread, lambda: transposes(r.aa, r.ab, r.xq2, near, far)])
+    sums = total(5, chan, packed(*gg, chan), [spread])
     norm_back(3, sums, chan)
     to_frames(3, r.time2, r.grad_pre)
-    shared_e3 = temporal_back(2, whole[3])
+    shared_e3 = temporal_back(2, whole[3], [lambda: transposes(r.aa, r.ab, r.xq2, near, far)])
     credit(1)
     gg = through_act(2, r.mid2, r.grad_mid, mid)
     shared_e3.wait()
@@ -1228,6 +1249,7 @@
         tile_mid=pltpu.VMEM((2, 4, CELL, mid), F32),
         tile_out=pltpu.VMEM((2, 4, CELL, chan), F32),
         back=pltpu.VMEM((2, CELL, mid), F32),
+        sum_flat=pltpu.VMEM((2, 2 * nb, 8, chan // 4), F32),
         norm_part=pltpu.VMEM((2, 8, mid), F32),
         sum_b=pltpu.VMEM((2, 4, 8, mid), F32),
         sum_c=pltpu.VMEM((2, nb // 2, 8, mid), F32),

time: 355 us -> 352 us (level)
  no operation moved by 1% of the time
where the time goes in v2:
time: 352 us; the launch traced here: 351 us
  Pallas kernels  328 us (93%)
  local copies, waits for them, and re-layouts  13.2 us (4%)
  other arithmetic  8.63 us (2%)
    pallas_call x1, Pallas kernels, per_device_fast(): pl.pallas_call(functools.partial(block_kernel, (nb, chan, mid, cell_count...  328 us

profile of v2, /device:TPU:3, one launch (start us, length us, event | category | flops | bytes accessed | tf_op | source)
XLA Modules:
  0.0 351.3 jit_solution(4073250479204000738)
XLA Ops:
  0.8 0.1 and_convert_fusion
  0.8 1.7 broadcast_multiply_fusion
  2.5 1.1 copy.29
  3.6 1.1 copy.30
  4.7 0.1 convert_bitcast_fusion.2
  4.8 0.7 broadcast_in_dim.5.all_refs_2_
  5.5 0.2 dynamic_update_slice.32
  5.7 0.2 dynamic_update_slice.33
  5.9 0.2 dynamic_update_slice.34
  6.1 0.2 dynamic_update_slice.35
  6.3 0.2 dynamic_update_slice.36
  6.5 0.2 dynamic_update_slice.37
  6.7 0.2 dynamic_update_slice.38
  6.9 0.2 dynamic_update_slice.39
  7.1 0.7 stack.38.all_refs_3_
  7.7 328.4 %shard_map.254 = (bf16[4,4,32,512]{3,2,1,0:T(8,128)(2,1)}, bf16[4,4,32,512]{3,2,1,0:T(8,128)(2,1)}, f32[8,1152]{1,0:T(8,128)}, bf16[576,512]{1,0:T(8,128)(2,1)},...) custom-call(bf16[4,4,32,512]{3,2,1,0:T(8,128)(2,1)} %bitcast.54, ...), custom_call_target="tpu_custom_call" | custom-call | tf_op jit(solution)/shard_map/pallas_call | solution.py:1299
  336.2 1.2 convert_bitcast_fusion.1
  337.4 1.6 copy.31
  339.1 0.1 convert_bitcast_fusion
  339.2 1.6 copy.32
  340.9 1.7 maximum_convert_fusion
  342.6 0.6 constant_dynamic-slice_fusion.7
  343.3 0.6 constant_dynamic-slice_fusion.6
  343.9 1.0 maximum_convert_fusion.2
  345.0 0.6 fusion
  345.5 0.6 fusion.1
  346.1 1.7 maximum_convert_fusion.1
  347.8 0.6 constant_dynamic-slice_fusion.3
  348.5 0.6 constant_dynamic-slice_fusion.2
  349.1 1.0 maximum_convert_fusion.3
  350.1 0.6 fusion.2
  350.7 0.6 fusion.3
  (50 shorter events, 0.2 us)
Async XLA Ops:
  0.6 4.1 %copy-start.16 = (s32[2,16]{1,0:T(2,128)S(1)}, s32[2,16]{1,0:T(2,128)}, u32[]{:S(2)}) copy-start(s32[2,16]{1,0:T(2,128)} %param.16) | copy-start | bytes 388
  0.7 4.8 %copy-start.8 = (bf16[144]{0:T(256)(128)(2,1)S(1)}, bf16[144]{0:T(256)(128)(2,1)}, u32[]{:S(2)}) copy-start(bf16[144]{0:T(256)(128)(2,1)} %param.19) | copy-start | bytes 868
  0.7 4.8 %copy-start.9 = (bf16[144]{0:T(256)(128)(2,1)S(1)}, bf16[144]{0:T(256)(128)(2,1)}, u32[]{:S(2)}) copy-start(bf16[144]{0:T(256)(128)(2,1)} %param.18) | copy-start | bytes 868
  0.7 5.2 %copy-start.10 = (bf16[64]{0:T(256)(128)(2,1)S(1)}, bf16[64]{0:T(256)(128)(2,1)}, u32[]{:S(2)}) copy-start(bf16[64]{0:T(256)(128)(2,1)} %param.22) | copy-start | bytes 388
  0.7 5.2 %copy-start.11 = (bf16[64]{0:T(256)(128)(2,1)S(1)}, bf16[64]{0:T(256)(128)(2,1)}, u32[]{:S(2)}) copy-start(bf16[64]{0:T(256)(128)(2,1)} %param.21) | copy-start | bytes 388
  0.7 5.6 %copy-start.12 = (bf16[144]{0:T(256)(128)(2,1)S(1)}, bf16[144]{0:T(256)(128)(2,1)}, u32[]{:S(2)}) copy-start(bf16[144]{0:T(256)(128)(2,1)} %param.25) | copy-start | bytes 868
  0.7 5.6 %copy-start.13 = (bf16[144]{0:T(256)(128)(2,1)S(1)}, bf16[144]{0:T(256)(128)(2,1)}, u32[]{:S(2)}) copy-start(bf16[144]{0:T(256)(128)(2,1)} %param.24) | copy-start | bytes 868
  0.7 5.9 %copy-start.14 = (bf16[64]{0:T(256)(128)(2,1)S(1)}, bf16[64]{0:T(256)(128)(2,1)}, u32[]{:S(2)}) copy-start(bf16[64]{0:T(256)(128)(2,1)} %param.28) | copy-start | bytes 388
  0.7 5.9 %copy-start.15 = (bf16[64]{0:T(256)(128)(2,1)S(1)}, bf16[64]{0:T(256)(128)(2,1)}, u32[]{:S(2)}) copy-start(bf16[64]{0:T(256)(128)(2,1)} %param.27) | copy-start | bytes 388
  336.2 2.9 copy-start.4
  337.4 3.5 copy-start.1
  337.4 3.5 copy-start.3
  339.2 3.4 copy-start.7
  339.2 4.7 %copy-start.6 = (bf16[2,432,256]{2,1,0:T(8,128)(2,1)S(1)}, bf16[2,432,256]{2,1,0:T(8,128)(2,1)}, u32[]{:S(2)}) copy-start(bf16[2,432,256]{2,1,0:T(8,128)(2,1)} %get-tuple-element.28) | copy-start | bytes 1327108
  340.9 5.2 %copy-start = (bf16[576,640]{1,0:T(8,128)(2,1)S(1)}, bf16[576,640]{1,0:T(8,128)(2,1)}, u32[]{:S(2)}) copy-start(bf16[576,640]{1,0:T(8,128)(2,1)} %get-tuple-element.30) | copy-start | bytes 2211844
  340.9 5.2 %copy-start.2 = (bf16[576,512]{1,0:T(8,128)(2,1)S(1)}, bf16[576,512]{1,0:T(8,128)(2,1)}, u32[]{:S(2)}) copy-start(bf16[576,512]{1,0:T(8,128)(2,1)} %get-tuple-element.29) | copy-start | bytes 1769476
  343.9 5.2 %copy-start.5 = (bf16[2,432,256]{2,1,0:T(8,128)(2,1)S(1)}, bf16[2,432,256]{2,1,0:T(8,128)(2,1)}, u32[]{:S(2)}) copy-start(bf16[2,432,256]{2,1,0:T(8,128)(2,1)} %get-tuple-element.31) | copy-start | bytes 1327108

commit v3 on v2

--- a/solution.py
+++ b/solution.py
@@ -460,7 +460,7 @@
     def shifted(i):
         before = by_lanes(r.down, rows_of(i * CHUNK, CHUNK + CELL))[CELL - 1 : CELL - 1 + CHUNK]
         after = by_lanes(r.up, rows_of(i * CHUNK, CHUNK + CELL))[1 : 1 + CHUNK]
-        gate = r.gate[...][None]
+        gate = r.param_in[CELL : 2 * CELL, 0:chan][None]
         return (before.reshape(2, CELL, chan) * gate, after.reshape(2, CELL, chan))
 
     def both_halves(weight, start, size):
@@ -471,7 +471,7 @@
         put_lanes(r.down, pl.ds(CELL, ROWS), nn(v[...], both_halves(weight, 0, mid)))
         copies = send_frames(k, (0,))
         y2 = nn(v[...], both_halves(weight, 2 * mid, mid))
-        y2 = (y2.reshape(ROWS // CELL, CELL, chan) * r.gate[...][None]).reshape(ROWS, chan)
+        y2 = (y2.reshape(ROWS // CELL, CELL, chan) * r.param_in[CELL : 2 * CELL, 0:chan][None]).reshape(ROWS, chan)
         put_lanes(r.up, pl.ds(0, ROWS), y2)
         copies += send_frames(k, (1,))
         out[...] = nn(v[...], both_halves(weight, mid, mid))
@@ -619,13 +619,16 @@
             both = jnp.concatenate([xq[1, c, rows, :], xq[2, c, rows, :]], axis=0)
             far[rows_of(row + j * quarter, quarter), 0 : 2 * ROWS] = both.T
 
-    def spatial_part(i, near, far, row, tap, n):
-        rows = rows_of(row, 3 * quarter)
+    def spatial_part(i, near, far, a, n):
+        size = mid // 2
+        rows = rows_of(a * size, size)
         acc = nn(near[rows, :], e_all[n][0 : 2 * ROWS, :])
         acc += nn(far[rows, :], e_all[n][2 * ROWS : 4 * ROWS, :])
         acc = acc.astype(BF16)
-        for j in range(6):
-            spare[n][gq(i, grad_row(tap + j // 2, j % 2), 64), :] = acc[64 * j : 64 * j + 64]
+        for j in range(size // 64):
+            part = a * (size // 64) + j
+            row = grad_row(lax.div(part, 2), lax.rem(part, 2))
+            spare[n][gq(i, row, 64), :] = acc[64 * j : 64 * j + 64]
 
     def transposes(xa, xb, xq, near, far):
         def body(a, _):
@@ -636,10 +639,10 @@
 
     def spatial_half(i, near, far, n):
         def body(a, _):
-            spatial_part(i, near, far, a * 3 * quarter, 3 * a, n)
+            spatial_part(i, near, far, a, n)
             return 0
 
-        lax.fori_loop(0, 3, body, 0)
+        lax.fori_loop(0, 2, body, 0)
 
     def transpose_v(v, sv):
         for c in range(mid // 128):
@@ -864,7 +867,7 @@
     xg, cg = r.x_grid, r.cot_grid
     tiles_start(r.x_tiles, xg, 0)
     gather_start(0)
-    r.param[...] = total(0, mid, r.param_in[...])
+    r.param[...] = total(0, mid, r.param_in[0:CELL, :])
     tiles_wait(r.x_tiles, xg, 0)
 
     def grid_chunk(ref, i):
@@ -1003,7 +1006,7 @@
             ef = e.astype(F32)
             put_e(1, i, e.reshape(CHUNK, chan))
             put_lanes(r.down, rows_of(i * CHUNK + CELL, CHUNK, CELL), ef.reshape(CHUNK, chan))
-            put_lanes(r.up, rows_of(i * CHUNK, CHUNK), (ef * r.gate[...][None]).reshape(CHUNK, chan))
+            put_lanes(r.up, rows_of(i * CHUNK, CHUNK), (ef * r.param_in[CELL : 2 * CELL, 0:chan][None]).reshape(CHUNK, chan))
             return 0
 
         loop(CHUNKS, body, 0)
@@ -1089,15 +1092,14 @@
     spatial_half(0, near, far, 0)
     reduce_start(0, 0)
     reduce_middle(1, 0)
-
-    def pass_on(k):
-        pl.when(k == 2)(lambda: share_e_on(1, 1))
-
-    conv_back(r.ea, r.eb, whole[0], r.grad_mid, pass_on)
+    share_e_on(1, 1)
+    for n in (0, 1):
+        reduce_last(2, n)
     share_e_wait(1, 1)
     spatial_half(0, near, far, 1)
     reduce_start(0, 1)
     reduce_middle(0, 0)
+    conv_back(r.ea, r.eb, whole[0], r.grad_mid)
 
     norm_copy = rc(r.norm_part.at[0], r.norm_part.at[1], r.norm_sem.at[0], r.norm_sem.at[1], beside)
     norm_copy.start()
@@ -1108,8 +1110,6 @@
 
     loop(CHUNKS, last_body, 0)
     send_tiles(out_grid, r.grad_input, 3)
-    for n in (0, 1):
-        reduce_last(2, n)
     reduce_last(1, 0)
     for n in (0, 1):
         final_on(2, n)
@@ -1166,7 +1166,7 @@
         return array.reshape(micro, frames, side, side, chan).astype(F32)
 
     gate = (1 - lax.dynamic_slice(starts, (w, h * few), (1, few))).astype(F32)
-    gate = jnp.broadcast_to(gate.reshape(few, 1), (few, chan))
+    gate = jnp.broadcast_to(gate.reshape(few, 1), (few, mid))
     here = jnp.where(h == 0, 1.0, 0.0)
 
     def placed(shard):
@@ -1194,8 +1194,7 @@
     inputs_of = dict(
         x_tiles=(tiles(inputs), pl.ANY),
         cot_tiles=(tiles(cotangent), pl.ANY),
-        gate=(gate, pltpu.VMEM),
-        param_in=(param, pltpu.VMEM),
+        param_in=(jnp.concatenate([param, gate], axis=0), pltpu.VMEM),
         first_spatial=(first_spatial, pl.ANY),
         first_temporal=(first_temporal, pl.ANY),
         second_spatial=(second_spatial, pl.ANY),

time: 352 us -> 353 us (level)
  no operation moved by 1% of the time
where the time goes in v3:
time: 353 us; the launch traced here: 349 us
  Pallas kernels  326 us (92%)
  local copies, waits for them, and re-layouts  13.2 us (4%)
  other arithmetic  8.64 us (2%)
    pallas_call x1, Pallas kernels, per_device_fast(): pl.pallas_call(functools.partial(block_kernel, (nb, chan, mid, cell_count...  326 us

profile of v3, /device:TPU:3, one launch (start us, length us, event | category | flops | bytes accessed | tf_op | source)
XLA Modules:
  0.0 349.0 jit_solution(9027300949717921873)
XLA Ops:
  0.8 0.1 and_convert_fusion
  0.8 1.7 broadcast_multiply_fusion
  2.5 1.1 copy.29
  3.6 1.1 copy.30
  4.7 0.2 dynamic_update_slice.32
  4.9 0.2 dynamic_update_slice.33
  5.2 0.2 dynamic_update_slice.34
  5.3 0.2 dynamic_update_slice.35
  5.5 0.2 dynamic_update_slice.36
  5.7 0.2 dynamic_update_slice.37
  6.0 0.2 dynamic_update_slice.38
  6.1 0.2 dynamic_update_slice.39
  6.3 0.1 convert_bitcast_fusion.2
  6.4 0.1 broadcast_in_dim.5
  6.5 1.3 concatenate.15.all_refs_2_
  7.8 326.1 %shard_map.254 = (bf16[4,4,32,512]{3,2,1,0:T(8,128)(2,1)}, bf16[4,4,32,512]{3,2,1,0:T(8,128)(2,1)}, f32[8,1152]{1,0:T(8,128)}, bf16[576,512]{1,0:T(8,128)(2,1)},...) custom-call(bf16[4,4,32,512]{3,2,1,0:T(8,128)(2,1)} %bitcast.52, ...), custom_call_target="tpu_custom_call" | custom-call | tf_op jit(solution)/shard_map/pallas_call | solution.py:1298
  333.9 1.2 convert_bitcast_fusion.1
  335.2 1.6 copy.31
  336.8 0.1 convert_bitcast_fusion
  336.9 1.6 copy.32
  338.6 1.7 maximum_convert_fusion
  340.3 0.6 constant_dynamic-slice_fusion.7
  341.0 0.6 constant_dynamic-slice_fusion.6
  341.7 1.0 maximum_convert_fusion.2
  342.7 0.6 fusion
  343.3 0.6 fusion.1
  343.8 1.7 maximum_convert_fusion.1
  345.5 0.6 constant_dynamic-slice_fusion.3
  346.2 0.6 constant_dynamic-slice_fusion.2
  346.8 1.0 maximum_convert_fusion.3
  347.9 0.6 fusion.2
  348.4 0.6 fusion.3
  (50 shorter events, 0.2 us)
Async XLA Ops:
  0.6 4.1 %copy-start.8 = (bf16[144]{0:T(256)(128)(2,1)S(1)}, bf16[144]{0:T(256)(128)(2,1)}, u32[]{:S(2)}) copy-start(bf16[144]{0:T(256)(128)(2,1)} %param.19) | copy-start | bytes 868
  0.7 4.1 %copy-start.9 = (bf16[144]{0:T(256)(128)(2,1)S(1)}, bf16[144]{0:T(256)(128)(2,1)}, u32[]{:S(2)}) copy-start(bf16[144]{0:T(256)(128)(2,1)} %param.18) | copy-start | bytes 868
  0.7 4.4 %copy-start.10 = (bf16[64]{0:T(256)(128)(2,1)S(1)}, bf16[64]{0:T(256)(128)(2,1)}, u32[]{:S(2)}) copy-start(bf16[64]{0:T(256)(128)(2,1)} %param.22) | copy-start | bytes 388
  0.7 4.4 %copy-start.11 = (bf16[64]{0:T(256)(128)(2,1)S(1)}, bf16[64]{0:T(256)(128)(2,1)}, u32[]{:S(2)}) copy-start(bf16[64]{0:T(256)(128)(2,1)} %param.21) | copy-start | bytes 388
  0.7 4.8 %copy-start.12 = (bf16[144]{0:T(256)(128)(2,1)S(1)}, bf16[144]{0:T(256)(128)(2,1)}, u32[]{:S(2)}) copy-start(bf16[144]{0:T(256)(128)(2,1)} %param.25) | copy-start | bytes 868
  0.7 4.8 %copy-start.13 = (bf16[144]{0:T(256)(128)(2,1)S(1)}, bf16[144]{0:T(256)(128)(2,1)}, u32[]{:S(2)}) copy-start(bf16[144]{0:T(256)(128)(2,1)} %param.24) | copy-start | bytes 868
  0.7 5.2 %copy-start.14 = (bf16[64]{0:T(256)(128)(2,1)S(1)}, bf16[64]{0:T(256)(128)(2,1)}, u32[]{:S(2)}) copy-start(bf16[64]{0:T(256)(128)(2,1)} %param.28) | copy-start | bytes 388
  0.7 5.2 %copy-start.15 = (bf16[64]{0:T(256)(128)(2,1)S(1)}, bf16[64]{0:T(256)(128)(2,1)}, u32[]{:S(2)}) copy-start(bf16[64]{0:T(256)(128)(2,1)} %param.27) | copy-start | bytes 388
  0.7 5.6 %copy-start.16 = (s32[2,16]{1,0:T(2,128)S(1)}, s32[2,16]{1,0:T(2,128)}, u32[]{:S(2)}) copy-start(s32[2,16]{1,0:T(2,128)} %param.16) | copy-start | bytes 388
  333.9 2.9 copy-start.4
  335.1 3.5 copy-start.1
  335.1 3.5 copy-start.3
  336.9 3.4 copy-start.7
  336.9 4.7 %copy-start.6 = (bf16[2,432,256]{2,1,0:T(8,128)(2,1)S(1)}, bf16[2,432,256]{2,1,0:T(8,128)(2,1)}, u32[]{:S(2)}) copy-start(bf16[2,432,256]{2,1,0:T(8,128)(2,1)} %get-tuple-element.28) | copy-start | bytes 1327108
  338.6 5.2 %copy-start = (bf16[576,640]{1,0:T(8,128)(2,1)S(1)}, bf16[576,640]{1,0:T(8,128)(2,1)}, u32[]{:S(2)}) copy-start(bf16[576,640]{1,0:T(8,128)(2,1)} %get-tuple-element.30) | copy-start | bytes 2211844
  338.6 5.2 %copy-start.2 = (bf16[576,512]{1,0:T(8,128)(2,1)S(1)}, bf16[576,512]{1,0:T(8,128)(2,1)}, u32[]{:S(2)}) copy-start(bf16[576,512]{1,0:T(8,128)(2,1)} %get-tuple-element.29) | copy-start | bytes 1769476
  341.6 5.2 %copy-start.5 = (bf16[2,432,256]{2,1,0:T(8,128)(2,1)S(1)}, bf16[2,432,256]{2,1,0:T(8,128)(2,1)}, u32[]{:S(2)}) copy-start(bf16[2,432,256]{2,1,0:T(8,128)(2,1)} %get-tuple-element.31) | copy-start | bytes 1327108
